TPU v7x, 32 devices: a whole 2x2x4 slice. The times are simulated.
32 devices in a mesh: head: 4 (over y, x), blk: 8 (over z, core).
Axes of the slice: x: 2, y: 2, z: 4, core: 2. Of those that a mesh axis runs over, the one named last changes fastest.
Arguments:
- tokens: bfloat16 [8, 2048, 768], P(None, ('head', 'blk')), may hold values from -6 to 6
- lengths: int32 [8], replicated, may hold values from 256 to 2048, as said below
- first_gain: bfloat16 [768], P(('head', 'blk')), may hold values from 0.25 to 1.75
- first_bias: bfloat16 [768], P(('head', 'blk')), may hold values from -1.25 to 1.25
- joint_weight: bfloat16 [768, 2304], P(('head', 'blk')), may hold values from -0.21875 to 0.21875
- query_bias: bfloat16 [768], P(('head', 'blk')), may hold values from -3 to 3
- value_bias: bfloat16 [768], P(('head', 'blk')), may hold values from -0.125 to 0.125
- output_weight: bfloat16 [768, 768], P(('head', 'blk')), may hold values from -6 to 6
- output_bias: bfloat16 [768], P(('head', 'blk')), may hold values from -1.25 to 1.25
- second_gain: bfloat16 [768], P(('head', 'blk')), may hold values from 0.25 to 1.75
- second_bias: bfloat16 [768], P(('head', 'blk')), may hold values from -1.25 to 1.25
- inner_weight: bfloat16 [768, 3072], P(('head', 'blk')), may hold values from -0.21875 to 0.21875
- inner_bias: bfloat16 [3072], P(('head', 'blk')), may hold values from -1.25 to 1.25
- outer_weight: bfloat16 [3072, 768], P(('head', 'blk')), may hold values from -0.4375 to 0.4375
- outer_bias: bfloat16 [768], P(('head', 'blk')), may hold values from -3 to 3
- cotangent: bfloat16 [8, 2048, 768], P(None, ('head', 'blk')), may hold values from -6 to 6
Outputs:
- output: bfloat16 [8, 2048, 768], P(None, ('head', 'blk'))
- tokens_gradient: bfloat16 [8, 2048, 768], P(None, ('head', 'blk'))
- first_gain_gradient: float32 [768], P(('head', 'blk'))
- first_bias_gradient: float32 [768], P(('head', 'blk'))
- joint_weight_gradient: float32 [768, 2304], P(('head', 'blk'))
- query_bias_gradient: float32 [768], P(('head', 'blk'))
- value_bias_gradient: float32 [768], P(('head', 'blk'))
- output_weight_gradient: float32 [768, 768], P(('head', 'blk'))
- output_bias_gradient: float32 [768], P(('head', 'blk'))
- second_gain_gradient: float32 [768], P(('head', 'blk'))
- second_bias_gradient: float32 [768], P(('head', 'blk'))
- inner_weight_gradient: float32 [768, 3072], P(('head', 'blk'))
- inner_bias_gradient: float32 [3072], P(('head', 'blk'))
- outer_weight_gradient: float32 [3072, 768], P(('head', 'blk'))
- outer_bias_gradient: float32 [768], P(('head', 'blk'))
- stats: float32 [3], replicated
Inputs may be any that keep to these rules, and one draw needn't show every extreme that they name: `lengths`: one slot, chosen by the seed, is full (2048).
All inputs are finite; a program needn't handle non-finite values.
Results may differ from a plain program's by a relative error of at most 0.02.
Values may be sent and summed in bfloat16 or wider, within the bound.
A program may use at most 128 MiB of HBM per device.

v0:
```python
import jax
import jax.numpy as jnp
from jax import lax
from jax.sharding import PartitionSpec as P

H = 12
DH = 64


EPS = 1e-12
NEG = -1e30


def passed_along(value, axis, steps):
    count = lax.axis_size(axis)
    pairs = [(source, (source + steps) % count) for source in range(count)]
    return lax.ppermute(value, axis, pairs)


def normalize(values, gain, shift):
    average = jnp.mean(values, axis=-1, keepdims=True)
    centered = values - average
    inverse = lax.rsqrt(jnp.mean(centered * centered, axis=-1, keepdims=True) + EPS)
    normed = centered * inverse
    return (normed * gain + shift, normed, inverse)


def normalize_back(incoming, normed, inverse, gain):
    scaled = incoming * gain
    inner = (
        scaled
        - jnp.mean(scaled, axis=-1, keepdims=True)
        - normed * jnp.mean(scaled * normed, axis=-1, keepdims=True)
    )
    return (
        inner * inverse,
        jnp.sum(incoming * normed, axis=(0, 1)),
        jnp.sum(incoming, axis=(0, 1)),
    )


def gelu_exact(values):
    return jax.nn.gelu(values, approximate=False)


def key_mask(lengths, source, piece_rows, block_count, head_count):
    rows_here = jnp.arange(head_count * piece_rows, dtype=jnp.int32)
    position = (
        rows_here // piece_rows * block_count + source
    ) * piece_rows + rows_here % piece_rows
    return position[None, :] < lengths[:, None]


def attend(query_part, state, keys_block, values_block, mask):
    best, total, running = state
    scores = jnp.einsum(
        "sqhd,skhd->sqhk", query_part, keys_block, preferred_element_type=jnp.float32
    ) * DH ** (-0.5)
    scores = jnp.where(mask[:, None, None, :], scores, NEG)
    fresh = jnp.maximum(best, jnp.max(scores, axis=-1))
    decay = jnp.exp(best - fresh)
    weights = jnp.exp(scores - fresh[..., None])
    total = total * decay + jnp.sum(weights, axis=-1)
    running = running * decay[..., None] + jnp.einsum(
        "sqhk,skhd->sqhd",
        weights.astype(jnp.bfloat16),
        values_block,
        preferred_element_type=jnp.float32,
    )
    return (fresh, total, running)


def block_grads(query_part, back_part, total_part, spread_part, keys_block, values_block, mask):
    scale = DH ** (-0.5)
    scores = (
        jnp.einsum("sqhd,skhd->sqhk", query_part, keys_block, preferred_element_type=jnp.float32)
        * scale
    )
    scores = jnp.where(mask[:, None, None, :], scores, NEG)
    chances = jnp.exp(scores - total_part[..., None])
    back_chances = jnp.einsum(
        "sqhd,skhd->sqhk", back_part, values_block, preferred_element_type=jnp.float32
    )
    back_scores = (chances * (back_chances - spread_part[..., None])).astype(jnp.bfloat16)
    query_step = (
        jnp.einsum("sqhk,skhd->sqhd", back_scores, keys_block, preferred_element_type=jnp.float32)
        * scale
    )
    key_step = (
        jnp.einsum("sqhk,sqhd->skhd", back_scores, query_part, preferred_element_type=jnp.float32)
        * scale
    )
    value_step = jnp.einsum(
        "sqhk,sqhd->skhd",
        chances.astype(jnp.bfloat16),
        back_part,
        preferred_element_type=jnp.float32,
    )
    return (query_step, key_step, value_step)


def on_device(
    tokens,
    lengths,
    first_gain,
    first_bias,
    joint_weight,
    query_bias,
    value_bias,
    output_weight,
    output_bias,
    second_gain,
    second_bias,
    inner_weight,
    inner_bias,
    outer_weight,
    outer_bias,
    cotangent,
):
    head_count = lax.axis_size("head")
    block_count = lax.axis_size("blk")
    block = lax.axis_index("blk")
    quarter = lax.axis_index("head")
    (
        gain_one,
        shift_one,
        joint_full,
        query_shift,
        value_shift,
        output_full,
        output_shift,
        gain_two,
        shift_two,
        inner_full,
        inner_shift,
        outer_full,
        outer_shift,
    ) = (
        lax.all_gather(first_gain, ("head", "blk"), axis=0, tiled=True),
        lax.all_gather(first_bias, ("head", "blk"), axis=0, tiled=True),
        lax.all_gather(joint_weight, ("head", "blk"), axis=0, tiled=True),
        lax.all_gather(query_bias, ("head", "blk"), axis=0, tiled=True),
        lax.all_gather(value_bias, ("head", "blk"), axis=0, tiled=True),
        lax.all_gather(output_weight, ("head", "blk"), axis=0, tiled=True),
        lax.all_gather(output_bias, ("head", "blk"), axis=0, tiled=True),
        lax.all_gather(second_gain, ("head", "blk"), axis=0, tiled=True),
        lax.all_gather(second_bias, ("head", "blk"), axis=0, tiled=True),
        lax.all_gather(inner_weight, ("head", "blk"), axis=0, tiled=True),
        lax.all_gather(inner_bias, ("head", "blk"), axis=0, tiled=True),
        lax.all_gather(outer_weight, ("head", "blk"), axis=0, tiled=True),
        lax.all_gather(outer_bias, ("head", "blk"), axis=0, tiled=True),
    )
    sequences, piece_rows, width = tokens.shape
    heads_here = H // head_count
    head_width = heads_here * DH
    rows = head_count * piece_rows
    shape_heads = (sequences, rows, heads_here, DH)
    shape_flat = (sequences, rows, head_width)
    own_position = (quarter * block_count + block) * piece_rows + jnp.arange(
        piece_rows, dtype=jnp.int32
    )
    valid = own_position[None, :] < lengths[:, None]
    keep = valid[..., None]
    inputs = tokens.astype(jnp.float32)
    gain_one_wide = gain_one.astype(jnp.float32)
    gain_two_wide = gain_two.astype(jnp.float32)
    first_out, first_unit, first_scale = normalize(
        inputs, gain_one_wide, shift_one.astype(jnp.float32)
    )
    first_low = first_out.astype(jnp.bfloat16)
    joint = jnp.einsum("scd,de->sce", first_low, joint_full, preferred_element_type=jnp.float32)
    query_flat = (joint[..., :width] + query_shift.astype(jnp.float32)).astype(jnp.bfloat16)
    key_flat = joint[..., width : 2 * width].astype(jnp.bfloat16)
    value_flat = (joint[..., 2 * width :] + value_shift.astype(jnp.float32)).astype(jnp.bfloat16)
    query_flat, key_flat, value_flat = (
        lax.all_to_all(query_flat, "head", split_axis=2, concat_axis=1, tiled=True),
        lax.all_to_all(key_flat, "head", split_axis=2, concat_axis=1, tiled=True),
        lax.all_to_all(value_flat, "head", split_axis=2, concat_axis=1, tiled=True),
    )
    query_rows = query_flat.reshape(shape_heads)
    key_rows = key_flat.reshape(shape_heads)
    value_rows = value_flat.reshape(shape_heads)

    def visit(carry):
        keys_block, values_block, source, state = carry
        keys_block, values_block = passed_along((keys_block, values_block), "blk", 1)
        source = (source - 1) % block_count
        mask = key_mask(lengths, source, piece_rows, block_count, head_count)
        return (
            keys_block,
            values_block,
            source,
            attend(query_rows, state, keys_block, values_block, mask),
        )

    start_state = (
        jnp.full((sequences, rows, heads_here), NEG, jnp.float32),
        jnp.zeros((sequences, rows, heads_here), jnp.float32),
        jnp.zeros(shape_heads, jnp.float32),
    )
    first_state = attend(
        query_rows,
        start_state,
        key_rows,
        value_rows,
        key_mask(lengths, block, piece_rows, block_count, head_count),
    )
    carry = (key_rows, value_rows, block, first_state)
    carry = lax.fori_loop(0, block_count // 2 - 1, lambda turn, state: visit(visit(state)), carry)
    best, total, running = visit(carry)[3]
    context = running / total[..., None]
    log_total = best + jnp.log(total)
    context_low = context.astype(jnp.bfloat16).reshape(shape_flat)
    context_tokens = lax.all_to_all(context_low, "head", split_axis=1, concat_axis=2, tiled=True)
    branch = jnp.einsum(
        "sce,ed->scd", context_tokens, output_full, preferred_element_type=jnp.float32
    ) + output_shift.astype(jnp.float32)
    residual = inputs + branch
    second_out, second_unit, second_scale = normalize(
        residual, gain_two_wide, shift_two.astype(jnp.float32)
    )
    second_low = second_out.astype(jnp.bfloat16)
    inner = jnp.einsum(
        "scd,df->scf", second_low, inner_full, preferred_element_type=jnp.float32
    ) + inner_shift.astype(jnp.float32)
    activated = gelu_exact(inner).astype(jnp.bfloat16)
    feed = jnp.einsum(
        "scf,fd->scd", activated, outer_full, preferred_element_type=jnp.float32
    ) + outer_shift.astype(jnp.float32)
    result = residual + feed
    output = jnp.where(keep, result, 0.0).astype(jnp.bfloat16)
    sums = lax.psum(
        (
            jnp.sum(jnp.where(keep, result * result, 0.0)),
            jnp.sum(jnp.where(keep, branch * branch, 0.0)),
            jnp.sum(jnp.where(keep, feed * feed, 0.0)),
        ),
        ("head", "blk"),
    )
    count = jnp.sum(lengths).astype(jnp.float32) * width
    stats = jnp.sqrt(jnp.stack(sums) / count + 1e-06)
    back_result = jnp.where(keep, cotangent.astype(jnp.float32), 0.0)
    back_feed = back_result.astype(jnp.bfloat16)
    outer_gradient = jnp.einsum(
        "scf,scd->fd", activated, back_feed, preferred_element_type=jnp.float32
    )
    outer_shift_gradient = jnp.sum(back_feed.astype(jnp.float32), axis=(0, 1))
    back_active = jnp.einsum(
        "scd,fd->scf", back_feed, outer_full, preferred_element_type=jnp.float32
    )
    back_inner = jax.vjp(gelu_exact, inner)[1](back_active)[0].astype(jnp.bfloat16)
    inner_gradient = jnp.einsum(
        "scd,scf->df", second_low, back_inner, preferred_element_type=jnp.float32
    )
    inner_shift_gradient = jnp.sum(back_inner.astype(jnp.float32), axis=(0, 1))
    back_second = jnp.einsum(
        "scf,df->scd", back_inner, inner_full, preferred_element_type=jnp.float32
    )
    back_norm_two, gain_two_gradient, shift_two_gradient = normalize_back(
        back_second, second_unit, second_scale, gain_two_wide
    )
    back_residual = back_result + back_norm_two
    back_branch = back_residual.astype(jnp.bfloat16)
    output_gradient = jnp.einsum(
        "sce,scd->ed", context_tokens, back_branch, preferred_element_type=jnp.float32
    )
    output_shift_gradient = jnp.sum(back_branch.astype(jnp.float32), axis=(0, 1))
    back_context = jnp.einsum(
        "scd,ed->sce", back_branch, output_full, preferred_element_type=jnp.float32
    ).astype(jnp.bfloat16)
    back_context = lax.all_to_all(back_context, "head", split_axis=2, concat_axis=1, tiled=True)
    back_heads = back_context.reshape(shape_heads)
    spread = jnp.sum(back_heads.astype(jnp.float32) * context, axis=-1)
    zero_heads = jnp.zeros(shape_heads, jnp.float32)

    def pass_keys(carry):
        keys_block, values_block, key_sum, value_sum, query_sum, source = carry
        mask = key_mask(lengths, source, piece_rows, block_count, head_count)
        query_step, key_step, value_step = block_grads(
            query_rows, back_heads, log_total, spread, keys_block, values_block, mask
        )
        keys_block, values_block = passed_along((keys_block, values_block), "blk", 1)
        key_sum, value_sum = passed_along((key_sum + key_step, value_sum + value_step), "blk", 1)
        return (
            keys_block,
            values_block,
            key_sum,
            value_sum,
            query_sum + query_step,
            (source - 1) % block_count,
        )

    carry = (key_rows, value_rows, zero_heads, zero_heads, zero_heads, block)
    carry = lax.fori_loop(
        0, block_count // 2, lambda turn, state: pass_keys(pass_keys(state)), carry
    )
    key_sum, value_sum, query_sum = (carry[2], carry[3], carry[4])
    back_query, back_key, back_value = (
        lax.all_to_all(
            query_sum.astype(jnp.bfloat16).reshape(shape_flat),
            "head",
            split_axis=1,
            concat_axis=2,
            tiled=True,
        ),
        lax.all_to_all(
            key_sum.astype(jnp.bfloat16).reshape(shape_flat),
            "head",
            split_axis=1,
            concat_axis=2,
            tiled=True,
        ),
        lax.all_to_all(
            value_sum.astype(jnp.bfloat16).reshape(shape_flat),
            "head",
            split_axis=1,
            concat_axis=2,
            tiled=True,
        ),
    )
    back_joint = jnp.concatenate([back_query, back_key, back_value], axis=-1)
    joint_gradient = jnp.einsum(
        "scd,sce->de", first_low, back_joint, preferred_element_type=jnp.float32
    )
    query_shift_gradient = jnp.sum(back_query.astype(jnp.float32), axis=(0, 1))
    value_shift_gradient = jnp.sum(back_value.astype(jnp.float32), axis=(0, 1))
    back_first = jnp.einsum(
        "sce,de->scd", back_joint, joint_full, preferred_element_type=jnp.float32
    )
    back_norm_one, gain_one_gradient, shift_one_gradient = normalize_back(
        back_first, first_unit, first_scale, gain_one_wide
    )
    tokens_gradient = (back_residual + back_norm_one).astype(jnp.bfloat16)
    shards = (
        lax.psum_scatter(gain_one_gradient, ("head", "blk"), scatter_dimension=0, tiled=True),
        lax.psum_scatter(shift_one_gradient, ("head", "blk"), scatter_dimension=0, tiled=True),
        lax.psum_scatter(joint_gradient, ("head", "blk"), scatter_dimension=0, tiled=True),
        lax.psum_scatter(query_shift_gradient, ("head", "blk"), scatter_dimension=0, tiled=True),
        lax.psum_scatter(value_shift_gradient, ("head", "blk"), scatter_dimension=0, tiled=True),
        lax.psum_scatter(output_gradient, ("head", "blk"), scatter_dimension=0, tiled=True),
        lax.psum_scatter(output_shift_gradient, ("head", "blk"), scatter_dimension=0, tiled=True),
        lax.psum_scatter(gain_two_gradient, ("head", "blk"), scatter_dimension=0, tiled=True),
        lax.psum_scatter(shift_two_gradient, ("head", "blk"), scatter_dimension=0, tiled=True),
        lax.psum_scatter(inner_gradient, ("head", "blk"), scatter_dimension=0, tiled=True),
        lax.psum_scatter(inner_shift_gradient, ("head", "blk"), scatter_dimension=0, tiled=True),
        lax.psum_scatter(outer_gradient, ("head", "blk"), scatter_dimension=0, tiled=True),
        lax.psum_scatter(outer_shift_gradient, ("head", "blk"), scatter_dimension=0, tiled=True),
    )
    return (
        output,
        tokens_gradient,
        shards[0],
        shards[1],
        shards[2],
        shards[3],
        shards[4],
        shards[5],
        shards[6],
        shards[7],
        shards[8],
        shards[9],
        shards[10],
        shards[11],
        shards[12],
        stats,
    )


def solution(mesh):
    in_specs = (
        P(None, ("head", "blk"), None),
        P(),
        P(("head", "blk")),
        P(("head", "blk")),
        P(("head", "blk"), None),
        P(("head", "blk")),
        P(("head", "blk")),
        P(("head", "blk"), None),
        P(("head", "blk")),
        P(("head", "blk")),
        P(("head", "blk")),
        P(("head", "blk"), None),
        P(("head", "blk")),
        P(("head", "blk"), None),
        P(("head", "blk")),
        P(None, ("head", "blk"), None),
    )
    out_specs = (
        P(None, ("head", "blk"), None),
        P(None, ("head", "blk"), None),
        P(("head", "blk")),
        P(("head", "blk")),
        P(("head", "blk"), None),
        P(("head", "blk")),
        P(("head", "blk")),
        P(("head", "blk"), None),
        P(("head", "blk")),
        P(("head", "blk")),
        P(("head", "blk")),
        P(("head", "blk"), None),
        P(("head", "blk")),
        P(("head", "blk"), None),
        P(("head", "blk")),
        P(),
    )
    return jax.shard_map(
        on_device, mesh=mesh, in_specs=in_specs, out_specs=out_specs, check_vma=False
    )
```

profile of v0, /device:TPU:0, one launch (start us, length us, event | category | flops | bytes accessed | tf_op | source)
XLA Modules:
  0.0 1342.2 jit_solution(305137427457584541)
XLA Ops:
  16.2 42.9 %all-reduce.19 = (bf16[768]{0:T(1024)(128)(2,1)S(1)}, bf16[768]{0:T(1024)(128)(2,1)S(1)}, bf16[768]{0:T(1024)(128)(2,1)S(1)}, bf16[768]{0:T(1024)(128)(2,1)S(1)}...) all-reduce(bf16[768]{0:T(1024)(128)(2,1)S(1)} %dynamic-update-slice, ...), channel_id=1, replica_groups=mesh['head'=4,'blk'=8] {'head','blk'}, use_global_device_ids=true, to_apply=%add.1 | all-reduce | flops 9216 | bytes 36864
  62.0 12.0 all-gather.5.cloned.1.call-done
  74.0 4.4 fusion.81
  94.4 4.7 all-to-all-done.2
  115.9 4.2 all-to-all-start.1
  143.3 4.6 bitcast_add_fusion.9
  147.9 141.7 %while.47 = (s32[]{:T(128)}, bf16[8,256,3,64]{1,3,2,0:T(8,128)(2,1)S(1)}, bf16[8,256,3,64]{1,3,2,0:T(8,128)(2,1)}, s32[]{:T(128)}, f32[8,256,3]{1,2,0:T(4,128)S(...) while((s32[]{:T(128)}, ...), condition=%wide.region_9.10_spmd, body=%wide.region_4.9_spmd.sunk | while | flops 841519104 | bytes 65147480 | solution.py:209
  149.0 12.8 collective-permute-done
  161.9 14.4 %collective-permute-done.2 = bf16[8,256,3,64]{1,3,2,0:T(8,128)(2,1)} collective-permute-done((bf16[8,256,3,64]{1,3,2,0:T(8,128)(2,1)}, bf16[8,256,3,64]{1,3,2,0:T(8,128)(2,1)}, u32[]{:S(2)}, u32[]{:S(2)}) %collective-permute-start.2) | collective-permute-done | bytes 786464 | tf_op jit(solution)/shard_map/while/body/eval_jaxpr/ppermute | solution.py:17
  178.9 5.7 collective-permute-done.1
  195.5 25.9 %collective-permute-done = bf16[8,256,3,64]{1,3,2,0:T(8,128)(2,1)} collective-permute-done((bf16[8,256,3,64]{1,3,2,0:T(8,128)(2,1)S(1)}, bf16[8,256,3,64]{1,3,2,0:T(8,128)(2,1)}, u32[]{:S(2)}, u32[]{:S(2)}) %collective-permute-start) | collective-permute-done | bytes 786464 | tf_op jit(solution)/shard_map/while/body/eval_jaxpr/ppermute | solution.py:17
  221.5 8.3 collective-permute-done.2
  232.4 5.7 collective-permute-done.1
  249.0 13.2 collective-permute-done
  262.3 8.3 collective-permute-done.2
  273.2 5.7 collective-permute-done.1
  289.7 10.3 collective-permute-start.13
  307.2 9.0 collective-permute-done.13
  316.2 3.9 fusion.143
  321.9 3.8 all-to-all-start.3
  325.8 9.3 all-to-all-done.3
  343.8 6.9 fusion.117
  353.3 15.4 %multiply_convert_fusion = (bf16[8,64,3072]{2,1,0:T(8,128)(2,1)}, f32[8,64,3072]{2,1,0:T(8,128)}) fusion(f32[8,64,3072]{2,1,0:T(8,128)S(1)} %get-tuple-element.535, f32[3072]{0:T(1024)S(1)} %convert_element_type.165, u8[64,3072]{1,0:T(8,128)(4,1)S(1)} %get-tuple-element.420, u8[64,3072]{1,0:T(8,128)(4,1)S(1)} %get-tuple-element.419), kind=kLoop, calls=%fused_computation.103 | loop fusion | flops 111673344 | bytes 16134144 | tf_op jit(solution)/shard_map/convert_element_type | solution.py:226
  368.7 9.4 convert_reduce_fusion
  378.1 6.2 fusion.75
  384.4 5.0 select_reduce_fusion.2
  399.8 3.8 convolution_bitcast_fusion.3
  403.7 4.1 all-to-all-done.4
  417.3 446.2 %while.48 = (s32[]{:T(128)}, bf16[8,256,3,64]{1,3,2,0:T(8,128)(2,1)}, bf16[8,256,3,64]{1,3,2,0:T(8,128)(2,1)}, f32[8,256,3,64]{1,3,2,0:T(8,128)}, f32[8,256,3,64...) while((s32[]{:T(128)}, ...), condition=%wide.region_18.19_spmd.clone, body=%wide.region_17.18_spmd.clone.sunk | while | flops 2049060864 | bytes 182617072 | solution.py:294
  424.5 3.7 bitcast_add_fusion.17
  431.5 5.3 collective-permute-start.10
  437.8 5.7 collective-permute-done.6
  447.0 13.3 collective-permute-done.8
  462.7 20.8 %collective-permute-done.10 = f32[8,256,3,64]{1,3,2,0:T(8,128)S(1)} collective-permute-done((f32[8,256,3,64]{1,3,2,0:T(8,128)S(1)}, f32[8,256,3,64]{1,3,2,0:T(8,128)S(1)}, u32[]{:S(2)}, u32[]{:S(2)}) %collective-permute-start.10) | collective-permute-done | bytes 1572896 | tf_op jit(solution)/shard_map/while/body/eval_jaxpr/ppermute | solution.py:17
  490.7 35.0 %collective-permute-done.5 = bf16[8,256,3,64]{1,3,2,0:T(8,128)(2,1)} collective-permute-done((bf16[8,256,3,64]{1,3,2,0:T(8,128)(2,1)S(1)}, bf16[8,256,3,64]{1,3,2,0:T(8,128)(2,1)}, u32[]{:S(2)}, u32[]{:S(2)}) %collective-permute-start.5) | collective-permute-done | bytes 786464 | tf_op jit(solution)/shard_map/while/body/eval_jaxpr/ppermute | solution.py:17
  525.7 8.3 collective-permute-done.7
  539.8 3.6 bitcast_add_fusion.17
  553.5 7.5 collective-permute-done.6
  564.4 13.3 collective-permute-done.8
  580.1 14.5 %collective-permute-done.10 = f32[8,256,3,64]{1,3,2,0:T(8,128)S(1)} collective-permute-done((f32[8,256,3,64]{1,3,2,0:T(8,128)S(1)}, f32[8,256,3,64]{1,3,2,0:T(8,128)S(1)}, u32[]{:S(2)}, u32[]{:S(2)}) %collective-permute-start.10) | collective-permute-done | bytes 1572896 | tf_op jit(solution)/shard_map/while/body/eval_jaxpr/ppermute | solution.py:17
  601.9 35.0 %collective-permute-done.5 = bf16[8,256,3,64]{1,3,2,0:T(8,128)(2,1)} collective-permute-done((bf16[8,256,3,64]{1,3,2,0:T(8,128)(2,1)S(1)}, bf16[8,256,3,64]{1,3,2,0:T(8,128)(2,1)}, u32[]{:S(2)}, u32[]{:S(2)}) %collective-permute-start.5) | collective-permute-done | bytes 786464 | tf_op jit(solution)/shard_map/while/body/eval_jaxpr/ppermute | solution.py:17
  636.8 8.3 collective-permute-done.7
  651.0 3.6 bitcast_add_fusion.17
  662.9 7.6 collective-permute-done.6
  674.0 13.3 collective-permute-done.8
  689.6 14.5 %collective-permute-done.10 = f32[8,256,3,64]{1,3,2,0:T(8,128)S(1)} collective-permute-done((f32[8,256,3,64]{1,3,2,0:T(8,128)S(1)}, f32[8,256,3,64]{1,3,2,0:T(8,128)S(1)}, u32[]{:S(2)}, u32[]{:S(2)}) %collective-permute-start.10) | collective-permute-done | bytes 1572896 | tf_op jit(solution)/shard_map/while/body/eval_jaxpr/ppermute | solution.py:17
  711.4 35.0 %collective-permute-done.5 = bf16[8,256,3,64]{1,3,2,0:T(8,128)(2,1)} collective-permute-done((bf16[8,256,3,64]{1,3,2,0:T(8,128)(2,1)S(1)}, bf16[8,256,3,64]{1,3,2,0:T(8,128)(2,1)}, u32[]{:S(2)}, u32[]{:S(2)}) %collective-permute-start.5) | collective-permute-done | bytes 786464 | tf_op jit(solution)/shard_map/while/body/eval_jaxpr/ppermute | solution.py:17
  746.4 8.3 collective-permute-done.7
  771.0 7.5 collective-permute-done.6
  782.0 13.3 collective-permute-done.8
  797.6 14.5 %collective-permute-done.10 = f32[8,256,3,64]{1,3,2,0:T(8,128)S(1)} collective-permute-done((f32[8,256,3,64]{1,3,2,0:T(8,128)S(1)}, f32[8,256,3,64]{1,3,2,0:T(8,128)S(1)}, u32[]{:S(2)}, u32[]{:S(2)}) %collective-permute-start.10) | collective-permute-done | bytes 1572896 | tf_op jit(solution)/shard_map/while/body/eval_jaxpr/ppermute | solution.py:17
  819.4 35.0 %collective-permute-done.5 = bf16[8,256,3,64]{1,3,2,0:T(8,128)(2,1)} collective-permute-done((bf16[8,256,3,64]{1,3,2,0:T(8,128)(2,1)S(1)}, bf16[8,256,3,64]{1,3,2,0:T(8,128)(2,1)}, u32[]{:S(2)}, u32[]{:S(2)}) %collective-permute-start.5) | collective-permute-done | bytes 786464 | tf_op jit(solution)/shard_map/while/body/eval_jaxpr/ppermute | solution.py:17
  854.3 8.3 collective-permute-done.7
  873.7 11.4 all-to-all-done.5
  885.1 3.7 all-to-all-start.6
  892.1 11.7 all-to-all-done.6
  928.1 5.2 convolution_bitcast_fusion.2
  934.7 7.2 convolution_bitcast_fusion.1
  943.1 8.4 convolution_bitcast_fusion
  953.8 6.3 fusion.110
  960.2 41.0 %all-reduce.18 = (f32[768]{0:T(1024)S(1)}, f32[768]{0:T(1024)S(1)}, f32[768]{0:T(1024)S(1)}, f32[768]{0:T(1024)S(1)}, f32[768]{0:T(1024)S(1)}, /*index=5*/f32[76...) all-reduce(f32[768]{0:T(1024)S(1)} %get-tuple-element.423, ...), channel_id=2, replica_groups=mesh['head'=4,'blk'=8] {'head','blk'}, use_global_device_ids=true, to_apply=%region_22.23.clone | all-reduce | flops 9219 | bytes 73752
  1011.8 39.9 %reduce-scatter.5.cloned.1.call-done = f32[24,2304]{1,0:T(8,128)} async-done(((f32[768,2304]{1,0:T(8,128)}), f32[24,2304]{1,0:T(8,128)}) %reduce-scatter.5.cloned.1.call-update) | async-done | bytes 221200 | tf_op jit(solution)/shard_map/reduce_scatter | solution.py:337
  1051.7 141.3 %reduce-scatter.9.cloned.1.call-done = f32[24,3072]{1,0:T(8,128)} async-done(((f32[768,3072]{1,0:T(8,128)}), f32[24,3072]{1,0:T(8,128)}) %reduce-scatter.9.cloned.1.call-update) | async-done | bytes 294928 | tf_op jit(solution)/shard_map/reduce_scatter | solution.py:344
  1193.0 142.1 %reduce-scatter.11.cloned.1.call-done = f32[96,768]{1,0:T(8,128)} async-done(((f32[3072,768]{1,0:T(8,128)}), f32[96,768]{1,0:T(8,128)}) %reduce-scatter.11.cloned.1.call-update) | async-done | bytes 294928 | tf_op jit(solution)/shard_map/reduce_scatter | solution.py:346
  (452 shorter events, 311.4 us)
Async XLA Ops:
  7.2 66.9 %all-gather.5.cloned.1.call-start = ((), (), s32[]{:S(2)}) async-start(), calls=%async_computation.12 | async-start | bytes 3649536 | tf_op jit(solution)/shard_map/all_gather | solution.py:141
  7.9 332.0 %all-gather.7.cloned.1.call-start = ((), (), s32[]{:S(2)}) async-start(), calls=%async_computation.13 | async-start | bytes 1216512 | tf_op jit(solution)/shard_map/all_gather | solution.py:144
  84.1 15.0 %all-to-all-start.2 = ((bf16[4,2,49152]{2,1,0:T(2,128)(2,1)}), bf16[4,2,49152]{2,1,0:T(2,128)(2,1)S(1)}, u32[]{:S(2)}, u32[]{:S(2)}) async-start(bf16[4,2,49152]{2,1,0:T(2,128)(2,1)} %reshape.418), calls=%async_computation.2 | async-start | bytes 1572864 | tf_op jit(solution)/shard_map/all_to_all | solution.py:176
  100.0 15.9 %all-to-all-start = ((bf16[4,2,49152]{2,1,0:T(2,128)(2,1)}), bf16[4,2,49152]{2,1,0:T(2,128)(2,1)S(1)}, u32[]{:S(2)}, u32[]{:S(2)}) async-start(bf16[4,2,49152]{2,1,0:T(2,128)(2,1)} %reshape.414), calls=%async_computation | async-start | bytes 1572864 | tf_op jit(solution)/shard_map/all_to_all | solution.py:177
  103.5 240.2 %all-gather.9.cloned.1.call-start = ((), (), s32[]{:S(2)}) async-start(), calls=%async_computation.14 | async-start | bytes 4866048 | tf_op jit(solution)/shard_map/all_gather | solution.py:148
  115.9 18.1 %all-to-all-start.1 = ((bf16[4,2,49152]{2,1,0:T(2,128)(2,1)}), bf16[4,2,49152]{2,1,0:T(2,128)(2,1)}, u32[]{:S(2)}, u32[]{:S(2)}) async-start(bf16[4,2,49152]{2,1,0:T(2,128)(2,1)} %reshape.416), calls=%async_computation.1 | async-start | bytes 1572864 | tf_op jit(solution)/shard_map/all_to_all | solution.py:178
  120.1 248.6 %all-gather.11.cloned.1.call-start = ((), (), s32[]{:S(2)}) async-start(), calls=%async_computation.15 | async-start | bytes 4866048 | tf_op jit(solution)/shard_map/all_gather | solution.py:150
  147.9 13.9 %collective-permute-start = (bf16[8,256,3,64]{1,3,2,0:T(8,128)(2,1)S(1)}, bf16[8,256,3,64]{1,3,2,0:T(8,128)(2,1)}, u32[]{:S(2)}, u32[]{:S(2)}) collective-permute-start(bf16[8,256,3,64]{1,3,2,0:T(8,128)(2,1)S(1)} %get-tuple-element.714), channel_id=1, source_target_pairs={{0,1},{1,2},{2,3},{3,4},{4,5},{5,6},{6,7},{7,0},{8,9},{9,10},{10,1... | collective-permute-start | bytes 2359304 | tf_op jit(solution)/shard_map/while/body/eval_jaxpr/ppermute | solution.py:17
  148.0 28.4 %collective-permute-start.2 = (bf16[8,256,3,64]{1,3,2,0:T(8,128)(2,1)}, bf16[8,256,3,64]{1,3,2,0:T(8,128)(2,1)}, u32[]{:S(2)}, u32[]{:S(2)}) collective-permute-start(bf16[8,256,3,64]{1,3,2,0:T(8,128)(2,1)} %get-tuple-element.715), channel_id=1, source_target_pairs={{0,1},{1,2},{2,3},{3,4},{4,5},{5,6},{6,7},{7,0},{8,9},{9,10},{10,1... | collective-permute-start | bytes 2359304 | tf_op jit(solution)/shard_map/while/body/eval_jaxpr/ppermute | solution.py:17
  161.8 22.9 %collective-permute-start.1 = (bf16[8,256,3,64]{1,3,2,0:T(8,128)(2,1)}, bf16[8,256,3,64]{1,3,2,0:T(8,128)(2,1)S(1)}, u32[]{:S(2)}, u32[]{:S(2)}) collective-permute-start(bf16[8,256,3,64]{1,3,2,0:T(8,128)(2,1)} %collective-permute-done), channel_id=1, source_target_pairs={{0,1},{1,2},{2,3},{3,4},{4,5},{5,6},{6,7},{7,0},{8,9},{9,10},{10,1... | collective-permute-start | bytes 2359304 | tf_op jit(solution)/shard_map/while/body/eval_jaxpr/ppermute | solution.py:17
  176.4 16.7 %collective-permute-start.3 = (bf16[8,256,3,64]{1,3,2,0:T(8,128)(2,1)}, bf16[8,256,3,64]{1,3,2,0:T(8,128)(2,1)S(1)}, u32[]{:S(2)}, u32[]{:S(2)}) collective-permute-start(bf16[8,256,3,64]{1,3,2,0:T(8,128)(2,1)} %collective-permute-done.2), channel_id=1, source_target_pairs={{0,1},{1,2},{2,3},{3,4},{4,5},{5,6},{6,7},{7,0},{8,9},{9,10},{10,1... | collective-permute-start | bytes 2359304 | tf_op jit(solution)/shard_map/while/body/eval_jaxpr/ppermute | solution.py:17
  195.3 26.1 %collective-permute-start = (bf16[8,256,3,64]{1,3,2,0:T(8,128)(2,1)S(1)}, bf16[8,256,3,64]{1,3,2,0:T(8,128)(2,1)}, u32[]{:S(2)}, u32[]{:S(2)}) collective-permute-start(bf16[8,256,3,64]{1,3,2,0:T(8,128)(2,1)S(1)} %get-tuple-element.714), channel_id=1, source_target_pairs={{0,1},{1,2},{2,3},{3,4},{4,5},{5,6},{6,7},{7,0},{8,9},{9,10},{10,1... | collective-permute-start | bytes 2359304 | tf_op jit(solution)/shard_map/while/body/eval_jaxpr/ppermute | solution.py:17
  195.4 34.4 %collective-permute-start.2 = (bf16[8,256,3,64]{1,3,2,0:T(8,128)(2,1)}, bf16[8,256,3,64]{1,3,2,0:T(8,128)(2,1)}, u32[]{:S(2)}, u32[]{:S(2)}) collective-permute-start(bf16[8,256,3,64]{1,3,2,0:T(8,128)(2,1)} %get-tuple-element.715), channel_id=1, source_target_pairs={{0,1},{1,2},{2,3},{3,4},{4,5},{5,6},{6,7},{7,0},{8,9},{9,10},{10,1... | collective-permute-start | bytes 2359304 | tf_op jit(solution)/shard_map/while/body/eval_jaxpr/ppermute | solution.py:17
  221.4 16.7 %collective-permute-start.1 = (bf16[8,256,3,64]{1,3,2,0:T(8,128)(2,1)}, bf16[8,256,3,64]{1,3,2,0:T(8,128)(2,1)S(1)}, u32[]{:S(2)}, u32[]{:S(2)}) collective-permute-start(bf16[8,256,3,64]{1,3,2,0:T(8,128)(2,1)} %collective-permute-done), channel_id=1, source_target_pairs={{0,1},{1,2},{2,3},{3,4},{4,5},{5,6},{6,7},{7,0},{8,9},{9,10},{10,1... | collective-permute-start | bytes 2359304 | tf_op jit(solution)/shard_map/while/body/eval_jaxpr/ppermute | solution.py:17
  229.9 16.7 %collective-permute-start.3 = (bf16[8,256,3,64]{1,3,2,0:T(8,128)(2,1)}, bf16[8,256,3,64]{1,3,2,0:T(8,128)(2,1)S(1)}, u32[]{:S(2)}, u32[]{:S(2)}) collective-permute-start(bf16[8,256,3,64]{1,3,2,0:T(8,128)(2,1)} %collective-permute-done.2), channel_id=1, source_target_pairs={{0,1},{1,2},{2,3},{3,4},{4,5},{5,6},{6,7},{7,0},{8,9},{9,10},{10,1... | collective-permute-start | bytes 2359304 | tf_op jit(solution)/shard_map/while/body/eval_jaxpr/ppermute | solution.py:17
  248.8 13.4 collective-permute-start
  248.9 21.7 %collective-permute-start.2 = (bf16[8,256,3,64]{1,3,2,0:T(8,128)(2,1)}, bf16[8,256,3,64]{1,3,2,0:T(8,128)(2,1)}, u32[]{:S(2)}, u32[]{:S(2)}) collective-permute-start(bf16[8,256,3,64]{1,3,2,0:T(8,128)(2,1)} %get-tuple-element.715), channel_id=1, source_target_pairs={{0,1},{1,2},{2,3},{3,4},{4,5},{5,6},{6,7},{7,0},{8,9},{9,10},{10,1... | collective-permute-start | bytes 2359304 | tf_op jit(solution)/shard_map/while/body/eval_jaxpr/ppermute | solution.py:17
  262.2 16.7 %collective-permute-start.1 = (bf16[8,256,3,64]{1,3,2,0:T(8,128)(2,1)}, bf16[8,256,3,64]{1,3,2,0:T(8,128)(2,1)S(1)}, u32[]{:S(2)}, u32[]{:S(2)}) collective-permute-start(bf16[8,256,3,64]{1,3,2,0:T(8,128)(2,1)} %collective-permute-done), channel_id=1, source_target_pairs={{0,1},{1,2},{2,3},{3,4},{4,5},{5,6},{6,7},{7,0},{8,9},{9,10},{10,1... | collective-permute-start | bytes 2359304 | tf_op jit(solution)/shard_map/while/body/eval_jaxpr/ppermute | solution.py:17
  270.6 16.7 %collective-permute-start.3 = (bf16[8,256,3,64]{1,3,2,0:T(8,128)(2,1)}, bf16[8,256,3,64]{1,3,2,0:T(8,128)(2,1)S(1)}, u32[]{:S(2)}, u32[]{:S(2)}) collective-permute-start(bf16[8,256,3,64]{1,3,2,0:T(8,128)(2,1)} %collective-permute-done.2), channel_id=1, source_target_pairs={{0,1},{1,2},{2,3},{3,4},{4,5},{5,6},{6,7},{7,0},{8,9},{9,10},{10,1... | collective-permute-start | bytes 2359304 | tf_op jit(solution)/shard_map/while/body/eval_jaxpr/ppermute | solution.py:17
  289.6 13.4 collective-permute-start.12
  289.7 26.5 %collective-permute-start.13 = (bf16[8,256,3,64]{1,3,2,0:T(8,128)(2,1)}, bf16[8,256,3,64]{1,3,2,0:T(8,128)(2,1)}, u32[]{:S(2)}, u32[]{:S(2)}) collective-permute-start(bf16[8,256,3,64]{1,3,2,0:T(8,128)(2,1)} %get-tuple-element.375), channel_id=1, source_target_pairs={{0,1},{1,2},{2,3},{3,4},{4,5},{5,6},{6,7},{7,0},{8,9},{9,10},{10,1... | collective-permute-start | bytes 2359304 | tf_op jit(solution)/shard_map/ppermute | solution.py:17
  321.9 13.2 all-to-all-start.3
  325.7 63.7 %copy-start.37 = (f32[768]{0:T(1024)}, f32[768]{0:T(1024)S(1)}, u32[]{:S(2)}) copy-start(f32[768]{0:T(1024)S(1)} %convert_element_type.162) | copy-start | bytes 9220
  325.8 63.5 %copy-start.46 = (pred[8,64]{1,0:T(8,128)(4,1)}, pred[8,64]{1,0:T(8,128)(4,1)S(1)}, u32[]{:S(2)}) copy-start(pred[8,64]{1,0:T(8,128)(4,1)S(1)} %broadcast_compare_fusion.6) | copy-start | bytes 1540
  396.3 11.5 all-to-all-start.4
  399.8 612.1 %reduce-scatter.7.cloned.1.call-start = ((), (), s32[]{:S(2)}) async-start(), calls=%async_computation.17 | async-start | bytes 2433024 | tf_op jit(solution)/shard_map/reduce_scatter | solution.py:340
  418.9 17.9 %collective-permute-start.4 = (bf16[8,256,3,64]{1,3,2,0:T(8,128)(2,1)S(1)}, bf16[8,256,3,64]{1,3,2,0:T(8,128)(2,1)S(1)}, u32[]{:S(2)}, u32[]{:S(2)}) collective-permute-start(bf16[8,256,3,64]{1,3,2,0:T(8,128)(2,1)S(1)} %copy.181), channel_id=1, source_target_pairs={{0,1},{1,2},{2,3},{3,4},{4,5},{5,6},{6,7},{7,0},{8,9},{9,10},{10,1... | collective-permute-start | bytes 2359304 | tf_op jit(solution)/shard_map/while/body/eval_jaxpr/ppermute | solution.py:17
  418.9 24.7 %collective-permute-start.6 = (bf16[8,256,3,64]{1,3,2,0:T(8,128)(2,1)}, bf16[8,256,3,64]{1,3,2,0:T(8,128)(2,1)}, u32[]{:S(2)}, u32[]{:S(2)}) collective-permute-start(bf16[8,256,3,64]{1,3,2,0:T(8,128)(2,1)} %get-tuple-element.760), channel_id=1, source_target_pairs={{0,1},{1,2},{2,3},{3,4},{4,5},{5,6},{6,7},{7,0},{8,9},{9,10},{10,1... | collective-permute-start | bytes 2359304 | tf_op jit(solution)/shard_map/while/body/eval_jaxpr/ppermute | solution.py:17
  428.2 32.1 %collective-permute-start.8 = (f32[8,256,3,64]{1,3,2,0:T(8,128)S(1)}, f32[8,256,3,64]{1,3,2,0:T(8,128)S(1)}, u32[]{:S(2)}, u32[]{:S(2)}) collective-permute-start(f32[8,256,3,64]{1,3,2,0:T(8,128)S(1)} %bitcast_add_fusion.17), channel_id=1, source_target_pairs={{0,1},{1,2},{2,3},{3,4},{4,5},{5,6},{6,7},{7,0},{8,9},{9,10},{10,1... | collective-permute-start | bytes 4718600 | tf_op jit(solution)/shard_map/while/body/eval_jaxpr/ppermute | solution.py:17
  431.5 51.9 %collective-permute-start.10 = (f32[8,256,3,64]{1,3,2,0:T(8,128)S(1)}, f32[8,256,3,64]{1,3,2,0:T(8,128)S(1)}, u32[]{:S(2)}, u32[]{:S(2)}) collective-permute-start(f32[8,256,3,64]{1,3,2,0:T(8,128)S(1)} %bitcast_add_fusion.19), channel_id=1, source_target_pairs={{0,1},{1,2},{2,3},{3,4},{4,5},{5,6},{6,7},{7,0},{8,9},{9,10},{10,1... | collective-permute-start | bytes 4718600 | tf_op jit(solution)/shard_map/while/body/eval_jaxpr/ppermute | solution.py:17
  462.7 71.4 %collective-permute-start.9 = (f32[8,256,3,64]{1,3,2,0:T(8,128)}, f32[8,256,3,64]{1,3,2,0:T(8,128)}, u32[]{:S(2)}, u32[]{:S(2)}) collective-permute-start(f32[8,256,3,64]{1,3,2,0:T(8,128)} %bitcast_add_fusion.18), channel_id=1, source_target_pairs={{0,1},{1,2},{2,3},{3,4},{4,5},{5,6},{6,7},{7,0},{8,9},{9,10},{10,1... | collective-permute-start | bytes 4718600 | tf_op jit(solution)/shard_map/while/body/eval_jaxpr/ppermute | solution.py:17
  486.4 47.6 %collective-permute-start.11 = (f32[8,256,3,64]{1,3,2,0:T(8,128)}, f32[8,256,3,64]{1,3,2,0:T(8,128)}, u32[]{:S(2)}, u32[]{:S(2)}) collective-permute-start(f32[8,256,3,64]{1,3,2,0:T(8,128)} %bitcast_add_fusion.20), channel_id=1, source_target_pairs={{0,1},{1,2},{2,3},{3,4},{4,5},{5,6},{6,7},{7,0},{8,9},{9,10},{10,1... | collective-permute-start | bytes 4718600 | tf_op jit(solution)/shard_map/while/body/eval_jaxpr/ppermute | solution.py:17
  486.4 39.3 %collective-permute-start.5 = (bf16[8,256,3,64]{1,3,2,0:T(8,128)(2,1)S(1)}, bf16[8,256,3,64]{1,3,2,0:T(8,128)(2,1)}, u32[]{:S(2)}, u32[]{:S(2)}) collective-permute-start(bf16[8,256,3,64]{1,3,2,0:T(8,128)(2,1)S(1)} %collective-permute-done.4), channel_id=1, source_target_pairs={{0,1},{1,2},{2,3},{3,4},{4,5},{5,6},{6,7},{7,0},{8,9},{9,10},{10,1... | collective-permute-start | bytes 2359304 | tf_op jit(solution)/shard_map/while/body/eval_jaxpr/ppermute | solution.py:17
  486.5 47.5 %collective-permute-start.7 = (bf16[8,256,3,64]{1,3,2,0:T(8,128)(2,1)}, bf16[8,256,3,64]{1,3,2,0:T(8,128)(2,1)S(1)}, u32[]{:S(2)}, u32[]{:S(2)}) collective-permute-start(bf16[8,256,3,64]{1,3,2,0:T(8,128)(2,1)} %collective-permute-done.6), channel_id=1, source_target_pairs={{0,1},{1,2},{2,3},{3,4},{4,5},{5,6},{6,7},{7,0},{8,9},{9,10},{10,1... | collective-permute-start | bytes 2359304 | tf_op jit(solution)/shard_map/while/body/eval_jaxpr/ppermute | solution.py:17
  536.1 16.4 %collective-permute-start.4 = (bf16[8,256,3,64]{1,3,2,0:T(8,128)(2,1)S(1)}, bf16[8,256,3,64]{1,3,2,0:T(8,128)(2,1)S(1)}, u32[]{:S(2)}, u32[]{:S(2)}) collective-permute-start(bf16[8,256,3,64]{1,3,2,0:T(8,128)(2,1)S(1)} %copy.181), channel_id=1, source_target_pairs={{0,1},{1,2},{2,3},{3,4},{4,5},{5,6},{6,7},{7,0},{8,9},{9,10},{10,1... | collective-permute-start | bytes 2359304 | tf_op jit(solution)/shard_map/while/body/eval_jaxpr/ppermute | solution.py:17
  536.1 24.9 %collective-permute-start.6 = (bf16[8,256,3,64]{1,3,2,0:T(8,128)(2,1)}, bf16[8,256,3,64]{1,3,2,0:T(8,128)(2,1)}, u32[]{:S(2)}, u32[]{:S(2)}) collective-permute-start(bf16[8,256,3,64]{1,3,2,0:T(8,128)(2,1)} %get-tuple-element.760), channel_id=1, source_target_pairs={{0,1},{1,2},{2,3},{3,4},{4,5},{5,6},{6,7},{7,0},{8,9},{9,10},{10,1... | collective-permute-start | bytes 2359304 | tf_op jit(solution)/shard_map/while/body/eval_jaxpr/ppermute | solution.py:17
  543.5 34.3 %collective-permute-start.8 = (f32[8,256,3,64]{1,3,2,0:T(8,128)S(1)}, f32[8,256,3,64]{1,3,2,0:T(8,128)S(1)}, u32[]{:S(2)}, u32[]{:S(2)}) collective-permute-start(f32[8,256,3,64]{1,3,2,0:T(8,128)S(1)} %bitcast_add_fusion.17), channel_id=1, source_target_pairs={{0,1},{1,2},{2,3},{3,4},{4,5},{5,6},{6,7},{7,0},{8,9},{9,10},{10,1... | collective-permute-start | bytes 4718600 | tf_op jit(solution)/shard_map/while/body/eval_jaxpr/ppermute | solution.py:17
  546.8 47.8 %collective-permute-start.10 = (f32[8,256,3,64]{1,3,2,0:T(8,128)S(1)}, f32[8,256,3,64]{1,3,2,0:T(8,128)S(1)}, u32[]{:S(2)}, u32[]{:S(2)}) collective-permute-start(f32[8,256,3,64]{1,3,2,0:T(8,128)S(1)} %bitcast_add_fusion.19), channel_id=1, source_target_pairs={{0,1},{1,2},{2,3},{3,4},{4,5},{5,6},{6,7},{7,0},{8,9},{9,10},{10,1... | collective-permute-start | bytes 4718600 | tf_op jit(solution)/shard_map/while/body/eval_jaxpr/ppermute | solution.py:17
  580.1 65.1 %collective-permute-start.9 = (f32[8,256,3,64]{1,3,2,0:T(8,128)}, f32[8,256,3,64]{1,3,2,0:T(8,128)}, u32[]{:S(2)}, u32[]{:S(2)}) collective-permute-start(f32[8,256,3,64]{1,3,2,0:T(8,128)} %bitcast_add_fusion.18), channel_id=1, source_target_pairs={{0,1},{1,2},{2,3},{3,4},{4,5},{5,6},{6,7},{7,0},{8,9},{9,10},{10,1... | collective-permute-start | bytes 4718600 | tf_op jit(solution)/shard_map/while/body/eval_jaxpr/ppermute | solution.py:17
  597.5 47.6 %collective-permute-start.11 = (f32[8,256,3,64]{1,3,2,0:T(8,128)}, f32[8,256,3,64]{1,3,2,0:T(8,128)}, u32[]{:S(2)}, u32[]{:S(2)}) collective-permute-start(f32[8,256,3,64]{1,3,2,0:T(8,128)} %bitcast_add_fusion.20), channel_id=1, source_target_pairs={{0,1},{1,2},{2,3},{3,4},{4,5},{5,6},{6,7},{7,0},{8,9},{9,10},{10,1... | collective-permute-start | bytes 4718600 | tf_op jit(solution)/shard_map/while/body/eval_jaxpr/ppermute | solution.py:17
  597.5 39.3 %collective-permute-start.5 = (bf16[8,256,3,64]{1,3,2,0:T(8,128)(2,1)S(1)}, bf16[8,256,3,64]{1,3,2,0:T(8,128)(2,1)}, u32[]{:S(2)}, u32[]{:S(2)}) collective-permute-start(bf16[8,256,3,64]{1,3,2,0:T(8,128)(2,1)S(1)} %collective-permute-done.4), channel_id=1, source_target_pairs={{0,1},{1,2},{2,3},{3,4},{4,5},{5,6},{6,7},{7,0},{8,9},{9,10},{10,1... | collective-permute-start | bytes 2359304 | tf_op jit(solution)/shard_map/while/body/eval_jaxpr/ppermute | solution.py:17
  597.6 47.5 %collective-permute-start.7 = (bf16[8,256,3,64]{1,3,2,0:T(8,128)(2,1)}, bf16[8,256,3,64]{1,3,2,0:T(8,128)(2,1)S(1)}, u32[]{:S(2)}, u32[]{:S(2)}) collective-permute-start(bf16[8,256,3,64]{1,3,2,0:T(8,128)(2,1)} %collective-permute-done.6), channel_id=1, source_target_pairs={{0,1},{1,2},{2,3},{3,4},{4,5},{5,6},{6,7},{7,0},{8,9},{9,10},{10,1... | collective-permute-start | bytes 2359304 | tf_op jit(solution)/shard_map/while/body/eval_jaxpr/ppermute | solution.py:17
  647.2 14.7 %collective-permute-start.4 = (bf16[8,256,3,64]{1,3,2,0:T(8,128)(2,1)S(1)}, bf16[8,256,3,64]{1,3,2,0:T(8,128)(2,1)S(1)}, u32[]{:S(2)}, u32[]{:S(2)}) collective-permute-start(bf16[8,256,3,64]{1,3,2,0:T(8,128)(2,1)S(1)} %copy.181), channel_id=1, source_target_pairs={{0,1},{1,2},{2,3},{3,4},{4,5},{5,6},{6,7},{7,0},{8,9},{9,10},{10,1... | collective-permute-start | bytes 2359304 | tf_op jit(solution)/shard_map/while/body/eval_jaxpr/ppermute | solution.py:17
  647.2 23.3 %collective-permute-start.6 = (bf16[8,256,3,64]{1,3,2,0:T(8,128)(2,1)}, bf16[8,256,3,64]{1,3,2,0:T(8,128)(2,1)}, u32[]{:S(2)}, u32[]{:S(2)}) collective-permute-start(bf16[8,256,3,64]{1,3,2,0:T(8,128)(2,1)} %get-tuple-element.760), channel_id=1, source_target_pairs={{0,1},{1,2},{2,3},{3,4},{4,5},{5,6},{6,7},{7,0},{8,9},{9,10},{10,1... | collective-permute-start | bytes 2359304 | tf_op jit(solution)/shard_map/while/body/eval_jaxpr/ppermute | solution.py:17
  654.6 32.7 %collective-permute-start.8 = (f32[8,256,3,64]{1,3,2,0:T(8,128)S(1)}, f32[8,256,3,64]{1,3,2,0:T(8,128)S(1)}, u32[]{:S(2)}, u32[]{:S(2)}) collective-permute-start(f32[8,256,3,64]{1,3,2,0:T(8,128)S(1)} %bitcast_add_fusion.17), channel_id=1, source_target_pairs={{0,1},{1,2},{2,3},{3,4},{4,5},{5,6},{6,7},{7,0},{8,9},{9,10},{10,1... | collective-permute-start | bytes 4718600 | tf_op jit(solution)/shard_map/while/body/eval_jaxpr/ppermute | solution.py:17
  657.9 46.3 %collective-permute-start.10 = (f32[8,256,3,64]{1,3,2,0:T(8,128)S(1)}, f32[8,256,3,64]{1,3,2,0:T(8,128)S(1)}, u32[]{:S(2)}, u32[]{:S(2)}) collective-permute-start(f32[8,256,3,64]{1,3,2,0:T(8,128)S(1)} %bitcast_add_fusion.19), channel_id=1, source_target_pairs={{0,1},{1,2},{2,3},{3,4},{4,5},{5,6},{6,7},{7,0},{8,9},{9,10},{10,1... | collective-permute-start | bytes 4718600 | tf_op jit(solution)/shard_map/while/body/eval_jaxpr/ppermute | solution.py:17
  689.6 65.1 %collective-permute-start.9 = (f32[8,256,3,64]{1,3,2,0:T(8,128)}, f32[8,256,3,64]{1,3,2,0:T(8,128)}, u32[]{:S(2)}, u32[]{:S(2)}) collective-permute-start(f32[8,256,3,64]{1,3,2,0:T(8,128)} %bitcast_add_fusion.18), channel_id=1, source_target_pairs={{0,1},{1,2},{2,3},{3,4},{4,5},{5,6},{6,7},{7,0},{8,9},{9,10},{10,1... | collective-permute-start | bytes 4718600 | tf_op jit(solution)/shard_map/while/body/eval_jaxpr/ppermute | solution.py:17
  707.1 47.6 %collective-permute-start.11 = (f32[8,256,3,64]{1,3,2,0:T(8,128)}, f32[8,256,3,64]{1,3,2,0:T(8,128)}, u32[]{:S(2)}, u32[]{:S(2)}) collective-permute-start(f32[8,256,3,64]{1,3,2,0:T(8,128)} %bitcast_add_fusion.20), channel_id=1, source_target_pairs={{0,1},{1,2},{2,3},{3,4},{4,5},{5,6},{6,7},{7,0},{8,9},{9,10},{10,1... | collective-permute-start | bytes 4718600 | tf_op jit(solution)/shard_map/while/body/eval_jaxpr/ppermute | solution.py:17
  707.1 39.3 %collective-permute-start.5 = (bf16[8,256,3,64]{1,3,2,0:T(8,128)(2,1)S(1)}, bf16[8,256,3,64]{1,3,2,0:T(8,128)(2,1)}, u32[]{:S(2)}, u32[]{:S(2)}) collective-permute-start(bf16[8,256,3,64]{1,3,2,0:T(8,128)(2,1)S(1)} %collective-permute-done.4), channel_id=1, source_target_pairs={{0,1},{1,2},{2,3},{3,4},{4,5},{5,6},{6,7},{7,0},{8,9},{9,10},{10,1... | collective-permute-start | bytes 2359304 | tf_op jit(solution)/shard_map/while/body/eval_jaxpr/ppermute | solution.py:17
  707.1 47.6 %collective-permute-start.7 = (bf16[8,256,3,64]{1,3,2,0:T(8,128)(2,1)}, bf16[8,256,3,64]{1,3,2,0:T(8,128)(2,1)S(1)}, u32[]{:S(2)}, u32[]{:S(2)}) collective-permute-start(bf16[8,256,3,64]{1,3,2,0:T(8,128)(2,1)} %collective-permute-done.6), channel_id=1, source_target_pairs={{0,1},{1,2},{2,3},{3,4},{4,5},{5,6},{6,7},{7,0},{8,9},{9,10},{10,1... | collective-permute-start | bytes 2359304 | tf_op jit(solution)/shard_map/while/body/eval_jaxpr/ppermute | solution.py:17
  756.8 13.2 collective-permute-start.4
  756.8 21.7 %collective-permute-start.6 = (bf16[8,256,3,64]{1,3,2,0:T(8,128)(2,1)}, bf16[8,256,3,64]{1,3,2,0:T(8,128)(2,1)}, u32[]{:S(2)}, u32[]{:S(2)}) collective-permute-start(bf16[8,256,3,64]{1,3,2,0:T(8,128)(2,1)} %get-tuple-element.760), channel_id=1, source_target_pairs={{0,1},{1,2},{2,3},{3,4},{4,5},{5,6},{6,7},{7,0},{8,9},{9,10},{10,1... | collective-permute-start | bytes 2359304 | tf_op jit(solution)/shard_map/while/body/eval_jaxpr/ppermute | solution.py:17
  764.2 31.1 %collective-permute-start.8 = (f32[8,256,3,64]{1,3,2,0:T(8,128)S(1)}, f32[8,256,3,64]{1,3,2,0:T(8,128)S(1)}, u32[]{:S(2)}, u32[]{:S(2)}) collective-permute-start(f32[8,256,3,64]{1,3,2,0:T(8,128)S(1)} %bitcast_add_fusion.17), channel_id=1, source_target_pairs={{0,1},{1,2},{2,3},{3,4},{4,5},{5,6},{6,7},{7,0},{8,9},{9,10},{10,1... | collective-permute-start | bytes 4718600 | tf_op jit(solution)/shard_map/while/body/eval_jaxpr/ppermute | solution.py:17
  767.4 44.7 %collective-permute-start.10 = (f32[8,256,3,64]{1,3,2,0:T(8,128)S(1)}, f32[8,256,3,64]{1,3,2,0:T(8,128)S(1)}, u32[]{:S(2)}, u32[]{:S(2)}) collective-permute-start(f32[8,256,3,64]{1,3,2,0:T(8,128)S(1)} %bitcast_add_fusion.19), channel_id=1, source_target_pairs={{0,1},{1,2},{2,3},{3,4},{4,5},{5,6},{6,7},{7,0},{8,9},{9,10},{10,1... | collective-permute-start | bytes 4718600 | tf_op jit(solution)/shard_map/while/body/eval_jaxpr/ppermute | solution.py:17
  797.6 65.1 %collective-permute-start.9 = (f32[8,256,3,64]{1,3,2,0:T(8,128)}, f32[8,256,3,64]{1,3,2,0:T(8,128)}, u32[]{:S(2)}, u32[]{:S(2)}) collective-permute-start(f32[8,256,3,64]{1,3,2,0:T(8,128)} %bitcast_add_fusion.18), channel_id=1, source_target_pairs={{0,1},{1,2},{2,3},{3,4},{4,5},{5,6},{6,7},{7,0},{8,9},{9,10},{10,1... | collective-permute-start | bytes 4718600 | tf_op jit(solution)/shard_map/while/body/eval_jaxpr/ppermute | solution.py:17
  815.0 47.6 %collective-permute-start.11 = (f32[8,256,3,64]{1,3,2,0:T(8,128)}, f32[8,256,3,64]{1,3,2,0:T(8,128)}, u32[]{:S(2)}, u32[]{:S(2)}) collective-permute-start(f32[8,256,3,64]{1,3,2,0:T(8,128)} %bitcast_add_fusion.20), channel_id=1, source_target_pairs={{0,1},{1,2},{2,3},{3,4},{4,5},{5,6},{6,7},{7,0},{8,9},{9,10},{10,1... | collective-permute-start | bytes 4718600 | tf_op jit(solution)/shard_map/while/body/eval_jaxpr/ppermute | solution.py:17
  815.1 39.3 %collective-permute-start.5 = (bf16[8,256,3,64]{1,3,2,0:T(8,128)(2,1)S(1)}, bf16[8,256,3,64]{1,3,2,0:T(8,128)(2,1)}, u32[]{:S(2)}, u32[]{:S(2)}) collective-permute-start(bf16[8,256,3,64]{1,3,2,0:T(8,128)(2,1)S(1)} %collective-permute-done.4), channel_id=1, source_target_pairs={{0,1},{1,2},{2,3},{3,4},{4,5},{5,6},{6,7},{7,0},{8,9},{9,10},{10,1... | collective-permute-start | bytes 2359304 | tf_op jit(solution)/shard_map/while/body/eval_jaxpr/ppermute | solution.py:17
  815.1 47.5 %collective-permute-start.7 = (bf16[8,256,3,64]{1,3,2,0:T(8,128)(2,1)}, bf16[8,256,3,64]{1,3,2,0:T(8,128)(2,1)S(1)}, u32[]{:S(2)}, u32[]{:S(2)}) collective-permute-start(bf16[8,256,3,64]{1,3,2,0:T(8,128)(2,1)} %collective-permute-done.6), channel_id=1, source_target_pairs={{0,1},{1,2},{2,3},{3,4},{4,5},{5,6},{6,7},{7,0},{8,9},{9,10},{10,1... | collective-permute-start | bytes 2359304 | tf_op jit(solution)/shard_map/while/body/eval_jaxpr/ppermute | solution.py:17
  866.9 18.2 %all-to-all-start.5 = ((bf16[8,256,192]{2,0,1:T(8,128)(2,1)}), bf16[8,256,192]{2,0,1:T(8,128)(2,1)S(1)}, u32[]{:S(2)}, u32[]{:S(2)}) async-start(bf16[8,256,192]{2,0,1:T(8,128)(2,1)} %copy.112), calls=%async_computation.5 | async-start | bytes 2097152 | tf_op jit(solution)/shard_map/all_to_all | solution.py:299
  885.1 18.7 %all-to-all-start.6 = ((bf16[8,256,192]{2,0,1:T(8,128)(2,1)}), bf16[8,256,192]{2,0,1:T(8,128)(2,1)S(1)}, u32[]{:S(2)}, u32[]{:S(2)}) async-start(bf16[8,256,192]{2,0,1:T(8,128)(2,1)} %copy.115), calls=%async_computation.6 | async-start | bytes 2097152 | tf_op jit(solution)/shard_map/all_to_all | solution.py:306
  904.8 14.4 %all-to-all-start.7 = ((bf16[8,256,192]{2,0,1:T(8,128)(2,1)}), bf16[8,256,192]{2,0,1:T(8,128)(2,1)S(1)}, u32[]{:S(2)}, u32[]{:S(2)}) async-start(bf16[8,256,192]{2,0,1:T(8,128)(2,1)} %copy.118), calls=%async_computation.7 | async-start | bytes 2097152 | tf_op jit(solution)/shard_map/all_to_all | solution.py:313
  908.3 143.4 %reduce-scatter.5.cloned.1.call-start = ((), (), s32[]{:S(2)}) async-start(), calls=%async_computation.16 | async-start | bytes 7299072 | tf_op jit(solution)/shard_map/reduce_scatter | solution.py:337
  933.3 259.7 %reduce-scatter.9.cloned.1.call-start = ((), (), s32[]{:S(2)}) async-start(), calls=%async_computation.18 | async-start | bytes 9732096 | tf_op jit(solution)/shard_map/reduce_scatter | solution.py:344
  941.9 393.2 %reduce-scatter.11.cloned.1.call-start = ((), (), s32[]{:S(2)}) async-start(), calls=%async_computation.19 | async-start | bytes 9732096 | tf_op jit(solution)/shard_map/reduce_scatter | solution.py:346
  (78 other events, 736.8 us)
Sparse Core Ops, SparseCore 0:
  11.0 62.9 all-gather.4
  77.0 52.9 all-gather.6
  133.1 89.1 all-gather.8
  289.8 68.7 all-gather.10
  406.2 349.4 reduce-scatter.6
  933.4 118.2 reduce-scatter.4
  1058.2 134.7 reduce-scatter.8
  1200.5 134.5 reduce-scatter.10
where the time goes:
time: 1350 us; the launch traced here: 1340 us
  waiting for transfers between devices  821 us (61%)
  matrix products  204 us (15%)
  local copies, waits for them, and re-layouts  118 us (9%)
  blocking collectives  83.9 us (6%)
  starting transfers between devices  52.8 us (4%)
  other arithmetic  44.8 us (3%)
  between operations  15.9 us (1%)
    ppermute x46, waiting for transfers between devices, passed_along(): return lax.ppermute(value, axis, pairs)  442 us
    reduce_scatter x1, waiting for transfers between devices, on_device(): lax.psum_scatter(outer_gradient, ('head', 'blk'), scatter_dimension=0, ti...  142 us
    reduce_scatter x1, waiting for transfers between devices, on_device(): lax.psum_scatter(inner_gradient, ('head', 'blk'), scatter_dimension=0, ti...  141 us
    unnamed x2, blocking collectives  83.9 us
    unnamed x137, local copies, waits for them, and re-layouts  48.4 us
    reduce_scatter x1, waiting for transfers between devices, on_device(): lax.psum_scatter(joint_gradient, ('head', 'blk'), scatter_dimension=0, ti...  39.9 us
  transfers between devices with their start and end apart: 62, of which 46 were waited for; matrix products, arithmetic and copies ran while one was open for 23% of the time, Pallas kernels for 0%

commit v1 on v0

--- a/solution.py
+++ b/solution.py
@@ -1,6 +1,8 @@
 import jax
 import jax.numpy as jnp
 from jax import lax
+from jax.experimental import pallas as pl
+from jax.experimental.pallas import tpu as pltpu
 from jax.sharding import PartitionSpec as P
 
 H = 12
@@ -366,6 +368,694 @@
     )
 
 
+MESH = pl.DeviceIdType.MESH
+WIDTH = H * DH
+GROUP = 3 * DH
+NT = (((1,), (1,)), ((), ()))
+NN = (((1,), (0,)), ((), ()))
+
+
+def place():
+    head = lax.axis_index("head")
+    blk = lax.axis_index("blk")
+    return head // 2, lax.rem(head, 2), blk // 2, lax.rem(blk, 2)
+
+
+def at(y, x, z, c):
+    return (y * 2 + x, z * 2 + c)
+
+
+def number(y, x, z, c):
+    return y * 16 + x * 8 + z * 2 + c
+
+
+def column(t):
+    return t // 4, lax.rem(t, 4)
+
+
+def meet(peers):
+    barrier = pltpu.get_barrier_semaphore()
+    for peer in peers:
+        pl.semaphore_signal(barrier, inc=1, device_id=peer, device_id_type=MESH)
+    pl.semaphore_wait(barrier, len(peers))
+
+
+class Mover:
+    def __init__(self, send_sem, local_sem, anyone):
+        self.send_sem = send_sem
+        self.local_sem = local_sem
+        self.anyone = anyone
+        self.sent = []
+        self.local = []
+
+    def push(self, source, target, sem, device):
+        copy = pltpu.make_async_remote_copy(
+            src_ref=source,
+            dst_ref=target,
+            send_sem=self.send_sem.at[len(self.sent)],
+            recv_sem=sem,
+            device_id=device,
+            device_id_type=MESH,
+        )
+        copy.start()
+        self.sent.append(copy)
+
+    def keep(self, source, target):
+        copy = pltpu.make_async_copy(source, target, self.local_sem.at[len(self.local)])
+        copy.start()
+        self.local.append(copy)
+        return copy
+
+    def landed(self, target, sem):
+        pltpu.make_async_remote_copy(
+            src_ref=target,
+            dst_ref=target,
+            send_sem=self.send_sem.at[0],
+            recv_sem=sem,
+            device_id=self.anyone,
+            device_id_type=MESH,
+        ).wait_recv()
+
+    def finish(self):
+        for copy in self.sent:
+            copy.wait_send()
+        for copy in self.local:
+            copy.wait()
+
+
+def spread_kernel(
+    tokens, cotangent, wj, wo, wi, wu, small,
+    tok_all, cot_own, wj_all, wo_all, wi_all, wu_all, small_all,
+    send_sem, local_sem, tok_sem, cot_sem, weight_sem,
+):
+    y, x, z, c = place()
+    mine = number(y, x, z, c)
+    spot = y * 4 + z
+    other_core = at(y, x, z, 1 - c)
+    across = at(y, 1 - x, z, c)
+    y1, x1 = jnp.where(c == 0, y, 1 - y), jnp.where(c == 0, 1 - x, x)
+    y2, x2 = jnp.where(c == 0, 1 - y, y), jnp.where(c == 0, x, 1 - x)
+    first, second = at(y1, x1, z, c), at(y2, x2, z, c)
+    spots = [column(lax.rem(spot + k, 8)) for k in range(1, 8)]
+    peers = [at(yy, x, zz, c) for yy, zz in spots] + [across, other_core]
+    meet(peers)
+    move = Mover(send_sem, local_sem, other_core)
+    sources = (wj, wo, wi, wu, small)
+    wholes = (wj_all, wo_all, wi_all, wu_all, small_all)
+
+    for yy, zz in spots:
+        move.push(tokens.at[yy * 4 + zz], tok_all.at[mine], tok_sem.at[mine], at(yy, x, zz, c))
+    move.push(tokens.at[spot], tok_all.at[mine], tok_sem.at[mine], across)
+    move.push(tokens.at[spot], tok_all.at[mine], tok_sem.at[mine], other_core)
+    move.keep(tokens.at[spot], tok_all.at[mine])
+
+    def hand(block, own, device):
+        for i, (source, whole) in enumerate(zip(sources, wholes)):
+            move.push(
+                source if own else whole.at[block], whole.at[block], weight_sem.at[i, block], device
+            )
+
+    def arrive(block):
+        for i, whole in enumerate(wholes):
+            move.landed(whole.at[block], weight_sem.at[i, block])
+
+    for k in range(1, 4):
+        hand(mine, True, at(y, x, lax.rem(z + k, 4), c))
+    for source, whole in zip(sources, wholes):
+        move.keep(source, whole.at[mine])
+    hand(mine, True, first)
+    hand(mine, True, second)
+    hand(mine, True, other_core)
+    for yy, zz in spots:
+        move.push(cotangent.at[yy * 4 + zz], cot_own.at[spot], cot_sem.at[spot], at(yy, x, zz, c))
+    move.keep(cotangent.at[spot], cot_own.at[spot])
+
+    back_spots = [column(lax.rem(spot + 8 - k, 8)) for k in range(1, 8)]
+    for yy, zz in back_spots:
+        block = number(yy, x, zz, c)
+        move.landed(tok_all.at[block], tok_sem.at[block])
+        move.push(tok_all.at[block], tok_all.at[block], tok_sem.at[block], across)
+        move.push(tok_all.at[block], tok_all.at[block], tok_sem.at[block], other_core)
+    lines = [lax.rem(z + 4 - k, 4) for k in range(4)]
+    for zz in lines[1:]:
+        block = number(y, x, zz, c)
+        arrive(block)
+        hand(block, False, first)
+        hand(block, False, second)
+        hand(block, False, other_core)
+    for yy, zz in [(y, z)] + back_spots:
+        block = number(yy, 1 - x, zz, c)
+        move.landed(tok_all.at[block], tok_sem.at[block])
+        move.push(tok_all.at[block], tok_all.at[block], tok_sem.at[block], other_core)
+    for zz in lines:
+        block = number(y1, x1, zz, c)
+        arrive(block)
+        hand(block, False, second)
+        hand(block, False, other_core)
+    for yy, xx in ((y2, x2), (1 - y, 1 - x)):
+        for zz in lines:
+            block = number(yy, xx, zz, c)
+            arrive(block)
+            hand(block, False, other_core)
+    for yy, zz in [(y, z)] + back_spots:
+        for xx in (x, 1 - x):
+            block = number(yy, xx, zz, 1 - c)
+            move.landed(tok_all.at[block], tok_sem.at[block])
+    for yy, zz in back_spots:
+        move.landed(cot_own.at[yy * 4 + zz], cot_sem.at[yy * 4 + zz])
+    for yy in range(2):
+        for xx in range(2):
+            for zz in range(4):
+                arrive(number(yy, xx, zz, 1 - c))
+    move.finish()
+
+
+def comm_call(kernel, outs, args, sends, locals_, sems, scratch, ident, space=None):
+    space = space or [pltpu.HBM] * len(args)
+    return pl.pallas_call(
+        kernel,
+        out_shape=[jax.ShapeDtypeStruct(shape, dtype) for shape, dtype, _ in outs],
+        in_specs=[pl.BlockSpec(memory_space=one) for one in space],
+        out_specs=[pl.BlockSpec(memory_space=one) for _, _, one in outs],
+        scratch_shapes=[
+            pltpu.SemaphoreType.DMA((sends,)),
+            pltpu.SemaphoreType.DMA((max(locals_, 1),)),
+            *[pltpu.SemaphoreType.DMA(shape) for shape in sems],
+            *scratch,
+        ],
+        compiler_params=pltpu.CompilerParams(
+            collective_id=ident, has_side_effects=True, vmem_limit_bytes=56 * 1024 * 1024
+        ),
+    )(*args)
+
+
+def quad(x, c):
+    return [(lax.rem(x + dx, 2), lax.rem(c + dc, 2)) for dx, dc in ((0, 1), (1, 0), (1, 1))]
+
+
+def to_rows_kernel(source, target, send_sem, local_sem, recv_sem):
+    y, x, z, c = place()
+    mine = x * 2 + c
+    meet([at(y, xx, z, cc) for xx, cc in quad(x, c)])
+    move = Mover(send_sem, local_sem, at(y, x, z, 1 - c))
+    for xx, cc in quad(x, c)[::-1]:
+        for yy in range(2):
+            move.push(
+                source.at[yy, xx, :, cc], target.at[mine, yy], recv_sem.at[mine, yy], at(y, xx, z, cc)
+            )
+    for yy in range(2):
+        move.keep(source.at[yy, x, :, c], target.at[mine, yy])
+    for xx, cc in quad(x, c):
+        for yy in range(2):
+            move.landed(target.at[xx * 2 + cc, yy], recv_sem.at[xx * 2 + cc, yy])
+    move.finish()
+
+
+def to_heads_kernel(source, target, send_sem, local_sem, recv_sem):
+    y, x, z, c = place()
+    mine = x * 2 + c
+    meet([at(y, xx, z, cc) for xx, cc in quad(x, c)])
+    move = Mover(send_sem, local_sem, at(y, x, z, 1 - c))
+    for xx, cc in quad(x, c)[::-1]:
+        for yy in range(2):
+            move.push(
+                source.at[xx * 2 + cc, yy],
+                target.at[yy, x, :, c],
+                recv_sem.at[mine, yy],
+                at(y, xx, z, cc),
+            )
+    for yy in range(2):
+        move.keep(source.at[mine, yy], target.at[yy, x, :, c])
+    for xx, cc in quad(x, c):
+        for yy in range(2):
+            move.landed(target.at[yy, xx, :, cc], recv_sem.at[xx * 2 + cc, yy])
+    move.finish()
+
+
+def wide(value):
+    return value.astype(jnp.float32)
+
+
+def reduce_kernel(
+    go, gi, gu, gs, outgoing,
+    out_o, out_i, out_u, out_s, output,
+    send_sem, local_sem, sem1, sem2, sem3, sem4, sem_out,
+    *held,
+):
+    y, x, z, c = place()
+    spot = y * 4 + z
+    other_core = at(y, x, z, 1 - c)
+    across = at(y, 1 - x, z, c)
+    y1, x1 = jnp.where(c == 0, y, 1 - y), jnp.where(c == 0, 1 - x, x)
+    y2, x2 = jnp.where(c == 0, 1 - y, y), jnp.where(c == 0, x, 1 - x)
+    first, second = at(y1, x1, z, c), at(y2, x2, z, c)
+    spots = [column(lax.rem(spot + k, 8)) for k in range(1, 8)]
+    meet([at(yy, x, zz, c) for yy, zz in spots] + [across, other_core])
+    move = Mover(send_sem, local_sem, other_core)
+    parts = (gu, gi, go, gs)
+    results = (out_u, out_i, out_o, out_s)
+    r1, r2, r3, r4 = held[0:4], held[4:8], held[8:12], held[12:16]
+    own, near1, near2 = y * 2 + x, y1 * 2 + x1, y2 * 2 + x2
+    far = (1 - y) * 2 + 1 - x
+    order = (far, near1, near2, own)
+    for i in range(4):
+        for quarter in order:
+            move.push(
+                parts[i].at[quarter, :, 1 - c], r1[i].at[quarter], sem1.at[i, quarter], other_core
+            )
+    for yy, zz in spots:
+        move.push(outgoing.at[yy * 4 + zz], output.at[spot], sem_out.at[spot], at(yy, x, zz, c))
+    move.keep(outgoing.at[spot], output.at[spot])
+
+    def gather(i, quarter):
+        move.landed(r1[i].at[quarter], sem1.at[i, quarter])
+        r1[i][quarter] = (wide(r1[i][quarter]) + wide(parts[i][quarter, :, c])).astype(r1[i].dtype)
+
+    def stage2(i):
+        for slot, quarter in ((1, far), (0, near1)):
+            gather(i, quarter)
+            move.push(r1[i].at[quarter], r2[i].at[slot], sem2.at[i, slot], first)
+
+    def stage3(i):
+        gather(i, near2)
+        move.landed(r2[i].at[1], sem2.at[i, 1])
+        r1[i][near2] = (wide(r1[i][near2]) + wide(r2[i][1])).astype(r1[i].dtype)
+        move.push(r1[i].at[near2], r3[i], sem3.at[i], second)
+
+    def stage4(i):
+        gather(i, own)
+        move.landed(r2[i].at[0], sem2.at[i, 0])
+        move.landed(r3[i], sem3.at[i])
+        r1[i][own] = (wide(r1[i][own]) + wide(r2[i][0]) + wide(r3[i][...])).astype(r1[i].dtype)
+        for k in range(1, 4):
+            zz = lax.rem(z + k, 4)
+            move.push(r1[i].at[own, zz], r4[i].at[k - 1], sem4.at[i, k - 1], at(y, x, zz, c))
+
+    def stage5(i):
+        total = wide(r1[i][own, z])
+        for k in range(1, 4):
+            move.landed(r4[i].at[k - 1], sem4.at[i, k - 1])
+            total = total + wide(r4[i][k - 1])
+        results[i][...] = total
+
+    stages = (stage2, stage3, stage4, stage5)
+    for turn in range(7):
+        for depth in range(3, -1, -1):
+            i = turn - depth
+            if 0 <= i < 4:
+                stages[depth](i)
+    for k in range(1, 8):
+        t = lax.rem(spot + 8 - k, 8)
+        move.landed(output.at[t], sem_out.at[t])
+    move.finish()
+
+
+def last_kernel(
+    gj, bf, out_j, out_b,
+    send_sem, local_sem, sem_y, sem_z, sem_g, sem_c, sem_x,
+    ry, rz, sj, rc, rx,
+):
+    y, x, z, c = place()
+    other_core = at(y, x, z, 1 - c)
+    across = at(y, 1 - x, z, c)
+    down = at(1 - y, x, z, c)
+    line = [lax.rem(z + k, 4) for k in range(1, 4)]
+    group = quad(x, c)
+    meet([at(y, xx, z, cc) for xx, cc in group] + [down] + [at(y, x, zz, c) for zz in line])
+    move = Mover(send_sem, local_sem, other_core)
+    move.push(gj.at[1 - y], ry, sem_y, down)
+    quarters = [(yy, xx) for xx in (1 - x, x) for yy in range(2)]
+    for yy, xx in quarters:
+        move.push(bf.at[yy, xx, :, 1 - c], rc.at[yy, xx], sem_c.at[yy, xx], other_core)
+    for yy, xx in quarters[:2]:
+        move.landed(rc.at[yy, xx], sem_c.at[yy, xx])
+        rc[yy, xx] = (wide(rc[yy, xx]) + wide(bf[yy, xx, :, c])).astype(rc.dtype)
+        move.push(rc.at[yy, xx], rx.at[yy], sem_x.at[yy], across)
+    move.landed(ry, sem_y)
+    ry[...] = (wide(ry[...]) + wide(gj[y])).astype(ry.dtype)
+    for k in range(3):
+        move.push(ry.at[:, line[k]], rz.at[k], sem_z.at[k], at(y, x, line[k], c))
+    for yy, xx in quarters[2:]:
+        move.landed(rc.at[yy, xx], sem_c.at[yy, xx])
+    total = wide(ry[:, z])
+    for k in range(3):
+        move.landed(rz.at[k], sem_z.at[k])
+        total = total + wide(rz[k])
+    sj[...] = total
+    mine = x * 2 + c
+    for xx, cc in group:
+        move.push(sj.at[xx, cc], out_j.at[mine], sem_g.at[mine], at(y, xx, z, cc))
+    move.keep(sj.at[x, c], out_j.at[mine])
+    for yy in range(2):
+        move.landed(rx.at[yy], sem_x.at[yy])
+        out_b[yy] = wide(rc[yy, x]) + wide(bf[yy, x, :, c]) + wide(rx[yy])
+    for xx, cc in group:
+        move.landed(out_j.at[xx * 2 + cc], sem_g.at[xx * 2 + cc])
+    move.finish()
+
+
+def return_kernel(grads, small, out, small_all, send_sem, local_sem, sem_t, sem_s):
+    y, x, z, c = place()
+    spot = y * 4 + z
+    mine = number(y, x, z, c)
+    others = []
+    for k in range(1, 32):
+        t = lax.rem(mine + k, 32)
+        others.append((t, (t // 8, lax.rem(t, 8))))
+    meet([device for _, device in others])
+    move = Mover(send_sem, local_sem, at(y, x, z, 1 - c))
+    for k in range(1, 8):
+        yy, zz = column(lax.rem(spot + k, 8))
+        move.push(grads.at[yy * 4 + zz], out.at[spot], sem_t.at[spot], at(yy, x, zz, c))
+    move.keep(grads.at[spot], out.at[spot])
+    for t, device in others:
+        move.push(small.at[t], small_all.at[mine], sem_s.at[mine], device)
+    move.keep(small.at[mine], small_all.at[mine])
+    for k in range(1, 8):
+        t = lax.rem(spot + 8 - k, 8)
+        move.landed(out.at[t], sem_t.at[t])
+    for t, device in others:
+        move.landed(small_all.at[t], sem_s.at[t])
+    move.finish()
+
+
+def dot(a, b, dims=NN):
+    return lax.dot_general(a, b, dims, preferred_element_type=jnp.float32)
+
+
+ROWS = 256
+
+
+def attend_kernel(
+    length, tok, wj, gain, shift, query_shift, value_shift, first, query, key, value, context, context_turned, log_total
+):
+    rows = tok.shape[0]
+
+    def project(i, _):
+        here = pl.ds(i * ROWS, ROWS)
+        normed = normalize(wide(tok[here, :]), gain[...], shift[...])[0].astype(jnp.bfloat16)
+        first[here, :] = normed
+        joint = dot(normed, wj[...])
+        low_q = (joint[:, :GROUP] + query_shift[...]).astype(jnp.bfloat16)
+        low_k = joint[:, GROUP : 2 * GROUP].astype(jnp.bfloat16)
+        low_v = (joint[:, 2 * GROUP :] + value_shift[...]).astype(jnp.bfloat16)
+        for h in range(3):
+            query[h, here, :] = low_q[:, h * DH : (h + 1) * DH]
+            key[h, here, :] = low_k[:, h * DH : (h + 1) * DH]
+            value[h, here, :] = low_v[:, h * DH : (h + 1) * DH]
+        return 0
+
+    lax.fori_loop(0, rows // ROWS, project, 0)
+    keep = lax.broadcasted_iota(jnp.int32, (rows, 1), 0) < length[0]
+    eye = jnp.eye(DH, dtype=jnp.bfloat16)
+    for h in range(3):
+        turned = dot(eye, value[h], NT).astype(jnp.bfloat16)
+
+        def block(i, _):
+            here = pl.ds(i * ROWS, ROWS)
+            scores = dot(key[h], query[h, here, :], NT) * DH ** (-0.5)
+            scores = jnp.where(keep, scores, NEG)
+            best = jnp.max(scores, axis=0, keepdims=True)
+            weights = jnp.exp(scores - best)
+            total = jnp.sum(weights, axis=0, keepdims=True)
+            mixed = dot(turned, weights.astype(jnp.bfloat16)) / total
+            context_turned[h, :, here] = mixed
+            log_total[h, :, here] = best + jnp.log(total)
+            context[here, h * DH : (h + 1) * DH] = mixed.T.astype(jnp.bfloat16)
+            return 0
+
+        lax.fori_loop(0, rows // ROWS, block, 0)
+
+
+def attend_back_kernel(
+    length, query, key, value, back_context, context_turned, log_total, joint, key_sum, value_sum
+):
+    rows = query.shape[1]
+    scale = DH ** (-0.5)
+    keep = lax.broadcasted_iota(jnp.int32, (rows, 1), 0) < length[0]
+    eye = jnp.eye(DH, dtype=jnp.bfloat16)
+    for h in range(3):
+        turned = dot(eye, key[h], NT).astype(jnp.bfloat16)
+        key_sum[...] = jnp.zeros_like(key_sum)
+        value_sum[...] = jnp.zeros_like(value_sum)
+
+        def block(i, _):
+            here = pl.ds(i * ROWS, ROWS)
+            queries = query[h, here, :]
+            backs = back_context[here, h * DH : (h + 1) * DH]
+            scores = dot(key[h], queries, NT) * scale
+            scores = jnp.where(keep, scores, NEG)
+            chances = jnp.exp(scores - log_total[h, :, here])
+            spread = jnp.sum(dot(eye, backs, NT) * context_turned[h, :, here], axis=0, keepdims=True)
+            back_scores = (chances * (dot(value[h], backs, NT) - spread)).astype(jnp.bfloat16)
+            joint[here, h * DH : (h + 1) * DH] = (dot(turned, back_scores) * scale).T.astype(jnp.bfloat16)
+            key_sum[...] += dot(back_scores, queries)
+            value_sum[...] += dot(chances.astype(jnp.bfloat16), backs)
+            return 0
+
+        lax.fori_loop(0, rows // ROWS, block, 0)
+        joint[:, GROUP + h * DH : GROUP + (h + 1) * DH] = (key_sum[...] * scale).astype(jnp.bfloat16)
+        joint[:, 2 * GROUP + h * DH : 2 * GROUP + (h + 1) * DH] = value_sum[...].astype(jnp.bfloat16)
+
+
+def local_call(kernel, outs, args, scratch=(), smem=1):
+    return pl.pallas_call(
+        kernel,
+        out_shape=[jax.ShapeDtypeStruct(shape, dtype) for shape, dtype in outs],
+        in_specs=[pl.BlockSpec(memory_space=pltpu.SMEM)] * smem
+        + [pl.BlockSpec(memory_space=pltpu.VMEM)] * (len(args) - smem),
+        out_specs=[pl.BlockSpec(memory_space=pltpu.VMEM)] * len(outs),
+        scratch_shapes=list(scratch),
+        compiler_params=pltpu.CompilerParams(vmem_limit_bytes=56 * 1024 * 1024),
+    )(*args)
+
+
+def packed(vectors, blocks, dtype, tile):
+    rows = [jnp.pad(v.reshape(blocks, 1, -1), ((0, 0), (0, 0), (0, 128 - v.size // blocks))) for v in vectors]
+    whole = jnp.concatenate(rows, axis=1).astype(dtype)
+    return jnp.pad(whole, ((0, 0), (0, tile - whole.shape[1]), (0, 0)))
+
+
+def owner_device(
+    tokens,
+    lengths,
+    first_gain,
+    first_bias,
+    joint_weight,
+    query_bias,
+    value_bias,
+    output_weight,
+    output_bias,
+    second_gain,
+    second_bias,
+    inner_weight,
+    inner_bias,
+    outer_weight,
+    outer_bias,
+    cotangent,
+):
+    bf16, f32 = jnp.bfloat16, jnp.float32
+    y, x, z, c = place()
+    mine = x * 2 + c
+    slots, piece, width = tokens.shape
+    ff = inner_weight.shape[1]
+    small = packed(
+        [first_gain, first_bias, query_bias, value_bias, output_bias, second_gain, second_bias, outer_bias, inner_bias],
+        1, bf16, 16,
+    )[0]
+    hbm, vmem = pltpu.HBM, pltpu.VMEM
+    tok_all, cot_own, wj_all, wo_all, wi_all, wu_all, small_all = comm_call(
+        spread_kernel,
+        [
+            ((32, piece, width), bf16, hbm),
+            ((8, piece, width), bf16, hbm),
+            ((32,) + joint_weight.shape, bf16, hbm),
+            ((32,) + output_weight.shape, bf16, hbm),
+            ((32,) + inner_weight.shape, bf16, hbm),
+            ((32,) + outer_weight.shape, bf16, hbm),
+            ((32, 16, 128), bf16, hbm),
+        ],
+        (tokens, cotangent, joint_weight, output_weight, inner_weight, outer_weight, small),
+        200, 8, [(32,), (8,), (5, 32)], [], 0,
+    )
+    vectors = jnp.transpose(small_all[:, :8, :24], (1, 0, 2)).reshape(8, width).astype(f32)
+    inner_shift = small_all[:, 8, :96].reshape(1, ff).astype(f32)
+    gain_one, shift_one, query_shift, value_shift, output_shift, gain_two, shift_two, outer_shift = (
+        vectors[i : i + 1] for i in range(8)
+    )
+    length = lax.dynamic_slice(lengths, (y * 4 + z,), (1,))
+    joint_full = wj_all.reshape(width, 3, 4, GROUP)
+    joint_here = lax.dynamic_index_in_dim(joint_full, mine, 2, keepdims=False).reshape(width, 3 * GROUP)
+    rows_all = 32 * piece
+    tok_flat = tok_all.reshape(rows_all, width)
+    first_low, query, key, value, context, context_turned, log_total = local_call(
+        attend_kernel,
+        [
+            ((rows_all, width), bf16),
+            ((3, rows_all, DH), bf16),
+            ((3, rows_all, DH), bf16),
+            ((3, rows_all, DH), bf16),
+            ((rows_all, GROUP), bf16),
+            ((3, DH, rows_all), f32),
+            ((3, 1, rows_all), f32),
+        ],
+        (
+            length, tok_flat, joint_here, gain_one, shift_one,
+            lax.dynamic_slice(query_shift, (0, mine * GROUP), (1, GROUP)),
+            lax.dynamic_slice(value_shift, (0, mine * GROUP), (1, GROUP)),
+        ),
+    )
+    natural = (2, 2, 4, 2, piece)
+    (context_rows,) = comm_call(
+        to_rows_kernel,
+        [((4, 2, 4, piece, GROUP), bf16, hbm)],
+        (context.reshape(natural + (GROUP,)),),
+        6, 2, [(4, 2)], [], 1,
+    )
+    rows = 8 * piece
+    context_low = jnp.transpose(context_rows.reshape(4, rows, GROUP), (1, 0, 2)).reshape(rows, width)
+
+    def own_rows(whole):
+        whole = lax.dynamic_index_in_dim(whole.reshape(natural + (-1,)), x, 1, keepdims=False)
+        return lax.dynamic_index_in_dim(whole, c, 2, keepdims=False).reshape(rows, -1)
+
+    spots = jnp.arange(8, dtype=jnp.int32)
+    position = (
+        number(spots // 4, x, spots % 4, c)[:, None] * piece + jnp.arange(piece, dtype=jnp.int32)
+    ).reshape(rows, 1)
+    keep = position < length[0]
+    inputs = own_rows(tok_all).astype(f32)
+    output_full = wo_all.reshape(width, width)
+    inner_full = wi_all.reshape(width, ff)
+    outer_full = wu_all.reshape(ff, width)
+    branch = dot(context_low, output_full) + output_shift
+    residual = inputs + branch
+    second_out, second_unit, second_scale = normalize(residual, gain_two, shift_two)
+    second_low = second_out.astype(bf16)
+    inner = dot(second_low, inner_full) + inner_shift
+    activated = gelu_exact(inner).astype(bf16)
+    feed = dot(activated, outer_full) + outer_shift
+    result = residual + feed
+    output_here = jnp.where(keep, result, 0.0).astype(bf16)
+    sums = [jnp.sum(jnp.where(keep, item * item, 0.0)) for item in (result, branch, feed)]
+    back_result = jnp.where(keep, cot_own.reshape(rows, width).astype(f32), 0.0)
+    back_feed = back_result.astype(bf16)
+    turn = (((0,), (0,)), ((), ()))
+    outer_gradient = dot(activated, back_feed, turn).astype(bf16)
+    outer_shift_gradient = jnp.sum(back_feed.astype(f32), axis=0)
+    back_active = dot(back_feed, outer_full, NT)
+    back_inner = jax.vjp(gelu_exact, inner)[1](back_active)[0].astype(bf16)
+    inner_gradient = dot(second_low, back_inner, turn).astype(bf16)
+    inner_shift_gradient = jnp.sum(back_inner.astype(f32), axis=0)
+    back_second = dot(back_inner, inner_full, NT)
+    back_norm_two, gain_two_gradient, shift_two_gradient = normalize_back(
+        back_second[None], second_unit[None], second_scale[None], gain_two
+    )
+    back_residual = back_result + back_norm_two[0]
+    back_branch = back_residual.astype(bf16)
+    output_gradient = dot(context_low, back_branch, turn).astype(bf16)
+    output_shift_gradient = jnp.sum(back_branch.astype(f32), axis=0)
+    back_context = jnp.einsum(
+        "rd,ged->gre", back_branch, output_full.reshape(4, GROUP, width), preferred_element_type=f32
+    ).astype(bf16)
+    (back_heads,) = comm_call(
+        to_heads_kernel,
+        [(natural + (GROUP,), bf16, hbm)],
+        (back_context.reshape(4, 2, 4, piece, GROUP),),
+        6, 2, [(4, 2)], [], 2,
+    )
+    (back_joint,) = local_call(
+        attend_back_kernel,
+        [((rows_all, 3 * GROUP), bf16)],
+        (length, query, key, value, back_heads.reshape(rows_all, GROUP), context_turned, log_total),
+        scratch=[vmem((rows_all, DH), f32), vmem((rows_all, DH), f32)],
+    )
+    stat_row = jnp.broadcast_to(jnp.stack(sums), (32, 3)).reshape(-1)
+    small_one = packed(
+        [outer_shift_gradient, gain_two_gradient, shift_two_gradient, output_shift_gradient, inner_shift_gradient, stat_row],
+        32, f32, 8,
+    )
+    grid = (4, 4, 2)
+    owned = [
+        (output_gradient, output_weight.shape, bf16),
+        (inner_gradient, inner_weight.shape, bf16),
+        (outer_gradient, outer_weight.shape, bf16),
+        (small_one, (8, 128), f32),
+    ]
+    order = [owned[2], owned[1], owned[0], owned[3]]
+    out_o, out_i, out_u, out_s, output = comm_call(
+        reduce_kernel,
+        [(shape, f32, vmem) for _, shape, _ in owned] + [(tokens.shape, bf16, hbm)],
+        tuple(item.reshape(grid + shape) for item, shape, _ in owned)
+        + (output_here.reshape(8, piece, width),),
+        63, 1, [(4, 4), (4, 2), (4,), (4, 3), (8,)],
+        [vmem((4, 4) + shape, dtype) for _, shape, dtype in order]
+        + [vmem((2, 4) + shape, dtype) for _, shape, dtype in order]
+        + [vmem((4,) + shape, dtype) for _, shape, dtype in order]
+        + [vmem((3,) + shape, dtype) for _, shape, dtype in order],
+        3,
+        [vmem] * 4 + [hbm],
+    )
+    joint_gradient = dot(first_low, back_joint, turn).astype(bf16)
+    back_first_part = dot(back_joint, joint_here, NT).astype(bf16)
+    lead = joint_weight.shape[0]
+    joint_parts, back_first = comm_call(
+        last_kernel,
+        [((4, lead, 3 * GROUP), f32, vmem), ((2, 4, piece, width), f32, vmem)],
+        (joint_gradient.reshape(2, 2, 4, 2, lead, 3 * GROUP), back_first_part.reshape(natural + (width,))),
+        13, 1, [(), (3,), (4,), (2, 2), (2,)],
+        [
+            vmem((2, 4, 2, lead, 3 * GROUP), bf16),
+            vmem((3, 2, 2, lead, 3 * GROUP), bf16),
+            vmem((2, 2, lead, 3 * GROUP), f32),
+            vmem((2, 2, 4, piece, width), bf16),
+            vmem((2, 4, piece, width), bf16),
+        ],
+        4,
+        [vmem] * 2,
+    )
+    joint_shard = jnp.transpose(joint_parts.reshape(4, lead, 3, GROUP), (1, 2, 0, 3)).reshape(lead, 3 * width)
+    _, first_unit, first_scale = normalize(inputs, gain_one, shift_one)
+    back_norm_one, gain_one_gradient, shift_one_gradient = normalize_back(
+        back_first.reshape(1, rows, width), first_unit[None], first_scale[None], gain_one
+    )
+    grads_here = (back_residual + back_norm_one[0]).astype(bf16)
+    shifts = jnp.sum(back_joint.astype(f32), axis=0)
+    zero = jnp.zeros((width,), f32)
+    query_shift_gradient = lax.dynamic_update_slice(zero, shifts[:GROUP], (mine * GROUP,))
+    value_shift_gradient = lax.dynamic_update_slice(zero, shifts[2 * GROUP :], (mine * GROUP,))
+    small_two = packed(
+        [gain_one_gradient, shift_one_gradient, query_shift_gradient, value_shift_gradient], 32, f32, 8
+    )
+    tokens_gradient, small_back = comm_call(
+        return_kernel,
+        [(tokens.shape, bf16, hbm), ((32, 8, 128), f32, hbm)],
+        (grads_here.reshape(8, piece, width), small_two),
+        38, 2, [(8,), (32,)], [], 5,
+    )
+    late = jnp.sum(small_back, axis=0)
+    count = jnp.sum(lengths).astype(f32) * width
+    stats = jnp.sqrt(out_s[5, :3] / count + 1e-06)
+    return (
+        output,
+        tokens_gradient,
+        late[0, :lead],
+        late[1, :lead],
+        joint_shard,
+        late[2, :lead],
+        late[3, :lead],
+        out_o,
+        out_s[3, :lead],
+        out_s[1, :lead],
+        out_s[2, :lead],
+        out_i,
+        out_s[4, : inner_bias.shape[0]],
+        out_u,
+        out_s[0, :lead],
+        stats,
+    )
+
+
 def solution(mesh):
     in_specs = (
         P(None, ("head", "blk"), None),
@@ -403,6 +1093,8 @@
         P(("head", "blk")),
         P(),
     )
+    small_slice = dict(mesh.shape) == {"head": 4, "blk": 8}
+    device_work = owner_device if small_slice else on_device
     return jax.shard_map(
-        on_device, mesh=mesh, in_specs=in_specs, out_specs=out_specs, check_vma=False
-    )
+        device_work, mesh=mesh, in_specs=in_specs, out_specs=out_specs, check_vma=False
+    )

time: 1350 us -> 517 us (0.38)
  waiting for transfers between devices: 821 us -> 0 us
  Pallas kernels: 0 us -> 372 us
  matrix products: 204 us -> 69.6 us
  blocking collectives: 83.9 us -> 0 us
  local copies, waits for them, and re-layouts: 118 us -> 49.5 us
  starting transfers between devices: 52.8 us -> 0 us
  other arithmetic: 44.8 us -> 19.8 us
  between operations: 15.9 us -> 2.12 us
    ppermute x46 -> x0, waiting for transfers between devices: 442 us -> none  [passed_along(): return lax.ppermute(value, axis, pairs)]
    pallas_call x0 -> x8, Pallas kernels: none -> 372 us  [the longest x6 281 us: comm_call(): pl.pallas_call(kernel, out_shape=[jax.ShapeDtypeStruct(shape, dtype) for...]
    reduce_scatter x4 -> x0, waiting for transfers between devices: 323 us -> none  [the longest x1 142 us: on_device(): lax.psum_scatter(outer_gradient, ('head', 'blk'), scatter_dimension=0, ti...]
    dot_general x68 -> x11, matrix products: 204 us -> 69.6 us  [the longest x10 68 us: dot(): return lax.dot_general(a, b, dims, preferred_element_type=jnp.float32)]
    unnamed x2 -> x0, blocking collectives: 83.9 us -> none
    unnamed x137 -> x59, local copies, waits for them, and re-layouts: 48.4 us -> 4.8 us
    all_to_all x8 -> x0, waiting for transfers between devices: 41.2 us -> none  [the longest x1 11.7 us: on_device(): lax.all_to_all(key_sum.astype(jnp.bfloat16).reshape(shape_flat), 'head',...]
    all_to_all x14 -> x0, local copies, waits for them, and re-layouts: 29.6 us -> none  [the longest x2 6.03 us: on_device(): lax.all_to_all(key_sum.astype(jnp.bfloat16).reshape(shape_flat), 'head',...]
  transfers between devices with their start and end apart: 62 -> 0, of which waited for: 46 -> 0; matrix products, arithmetic and copies ran while one was open for 23% -> 0% of each run, Pallas kernels for 0% -> 0%
where the time goes in v1:
time: 517 us; the launch traced here: 513 us
  Pallas kernels  372 us (72%)
  matrix products  69.6 us (13%)
  local copies, waits for them, and re-layouts  49.5 us (10%)
  other arithmetic  19.8 us (4%)
    pallas_call x6, Pallas kernels, comm_call(): pl.pallas_call(kernel, out_shape=[jax.ShapeDtypeStruct(shape, dtype) for...  281 us
    pallas_call x2, Pallas kernels, local_call(): pl.pallas_call(kernel, out_shape=[jax.ShapeDtypeStruct(shape, dtype) for...  91.3 us
    dot_general x10, matrix products, dot(): return lax.dot_general(a, b, dims, preferred_element_type=jnp.float32)  68 us

profile of v1, /device:TPU:0, one launch (start us, length us, event | category | flops | bytes accessed | tf_op | source)
XLA Modules:
  0.0 513.4 jit_solution(5352509623605886442)
XLA Ops:
  0.7 1.2 dynamic_slice.19.length
  1.9 0.7 pad.76
  2.6 0.7 pad.77
  3.2 0.7 pad.78
  3.9 0.7 pad.79
  4.6 0.7 pad.80
  5.2 0.7 pad.81
  5.9 0.7 pad.82
  6.5 0.7 pad.83
  7.2 0.7 pad.84
  7.9 0.6 pad_bitcast_fusion.small
  8.5 107.7 %shard_map.279 = (bf16[32,64,768]{2,1,0:T(8,128)(2,1)}, bf16[8,64,768]{2,1,0:T(8,128)(2,1)}, bf16[32,24,2304]{2,1,0:T(8,128)(2,1)}, bf16[32,24,768]{2,1,0:T(8,12...) custom-call(bf16[8,64,768]{2,1,0:T(8,128)(2,1)} %tokens.1, ...), custom_call_target="tpu_custom_call" | custom-call | tf_op jit(solution)/shard_map/pallas_call | solution.py:535
  116.2 10.2 %reshape.533 = bf16[768,3,4,192]{3,2,1,0:T(4,128)(2,1)} reshape(bf16[32,24,2304]{2,1,0:T(8,128)(2,1)} %get-tuple-element.40) | data formatting | bytes 7077888 | tf_op jit(solution)/shard_map/reshape | solution.py:887
  126.4 4.8 constant_dynamic-slice_fusion.2
  131.2 4.4 copy.47
  135.6 2.2 copy.48.wj
  138.2 0.7 slice.86.gain
  138.9 0.7 slice.88.shift
  139.7 0.6 constant_dynamic-slice_fusion
  140.4 44.7 %shard_map.280 = (bf16[2048,768]{1,0:T(8,128)(2,1)}, bf16[3,2048,64]{2,1,0:T(8,128)(2,1)}, bf16[3,2048,64]{2,1,0:T(8,128)(2,1)}, bf16[3,2048,64]{2,1,0:T(8,128)(...) custom-call(s32[1]{0:T(128)} %dynamic_slice.19.length, ...), custom_call_target="tpu_custom_call" | custom-call | tf_op jit(solution)/shard_map/pallas_call | solution.py:822
  185.0 15.6 %shard_map.281 = bf16[4,2,4,64,192]{4,3,2,1,0:T(8,128)(2,1)} custom-call(bf16[2,2,4,2,64,192]{5,4,3,2,1,0:T(8,128)(2,1)} %bitcast.164), custom_call_target="tpu_custom_call" | custom-call | tf_op jit(solution)/shard_map/pallas_call | solution.py:535
  200.6 2.7 copy.49
  203.3 0.7 add_compare_fusion
  204.2 4.1 fusion.29
  208.6 1.7 multiply_reduce_fusion.5
  210.3 8.2 %fusion.26 = f32[512,3072]{1,0:T(8,128)} fusion(bf16[768,3072]{1,0:T(8,128)(2,1)} %bitcast.179, f32[512,768]{1,0:T(8,128)} %get-tuple-element.93, f32[768]{0:T(1024)S(1)} %add.249, f32[768]{0:T(1024)S(1)} %mul.220, f32[512]{0:T(512)S(1)} %add_rsqrt_fusion.1, f32[512]{0:T(512)S(1)} %broadcast_multiply_fusion.5), kind=kOutput, calls=%fused_computation.130 | convolution fusion | flops 2417885184 | bytes 12593152 | tf_op jit(solution)/shard_map/dot_general | solution.py:743
  218.6 1.4 convert_reduce_fusion.3
  220.0 18.7 %convert_reduce_fusion = (f32[3072]{0:T(1024)S(1)}, bf16[512,3072]{1,0:T(8,128)(2,1)S(1)}, f32[512,3072]{1,0:T(8,128)S(1)}) fusion(f32[512,3072]{1,0:T(8,128)} %fusion.26, f32[3072]{0:T(1024)S(1)} %reshape.565, bf16[512,768]{1,0:T(8,128)(2,1)S(1)} %bitcast.166, bf16[3072,768]{1,0:T(8,128)(2,1)} %bitcast.177), kind=kOutput, calls=%fused_computation.2 | convolution fusion | flops 2533880832 | bytes 21258240 | tf_op jit(solution)/shard_map/dot_general | solution.py:743
  238.8 6.2 %fusion.30 = f32[512,768]{1,0:T(8,128)S(1)} fusion(bf16[512,3072]{1,0:T(8,128)(2,1)S(1)} %get-tuple-element.85, bf16[768,3072]{1,0:T(8,128)(2,1)} %bitcast.180), kind=kOutput, calls=%fused_computation.132 | convolution fusion | flops 2415919104 | bytes 9437184 | tf_op jit(solution)/shard_map/dot_general | solution.py:743
  245.0 3.3 multiply_convert_fusion
  248.4 8.6 %select_reduce_fusion.2 = (f32[]{:T(128)}, f32[]{:T(128)}, f32[512]{0:T(512)S(1)}, f32[512]{0:T(512)S(1)}, f32[768]{0:T(1024)S(1)}, /*index=5*/f32[768]{0:T(1024)S(1)}, f32[]{:T(128)}, bf16[512,768]{1,0:T(8,128)(2,1)}) fusion(pred[512]{0:T(512)(128)(4,1)S(1)} %lt.48, f32[512,768]{1,0:T(8,128)S(1)} %copy-done.1, f32[768]{0:T(1024)S(1)} %add.255, ...), kind=kOutput, calls=%fused_computation.41 | convolution fusion | flops 2424567296 | bytes 13390348 | tf_op jit(solution)/shard_map/dot_general | solution.py:743
  256.9 1.8 convert_reduce_fusion.2
  258.7 1.8 convolution_convert_fusion.3
  260.5 0.8 copy-done.21
  261.3 4.8 convolution_convert_fusion.1
  266.2 4.6 convolution_convert_fusion
  271.2 2.0 select_maximum_fusion.3
  273.3 0.7 pad.93.clone
  274.0 82.7 %shard_map.282 = (f32[24,768]{1,0:T(8,128)}, f32[24,3072]{1,0:T(8,128)}, f32[96,768]{1,0:T(8,128)}, f32[8,128]{1,0:T(8,128)}, bf16[8,64,768]{2,1,0:T(8,128)(2,1)}) custom-call(bf16[4,4,2,24,768]{4,3,2,1,0:T(8,128)(2,1)} %bitcast.163, bf16[4,4,2,24,3072]{4,3,2,1,0:T(8,128)(2,1)} %bitcast.149, bf16[4,4,2,96,768]{4,3,2,1,0:T(8,128)(2,1)} %bitcast.150, ...), custom_call_target="tpu_custom_call" | custom-call | tf_op jit(solution)/shard_map/pallas_call | solution.py:535
  356.7 1.7 fusion.16
  358.4 2.2 copy.52
  360.6 15.5 %shard_map.283 = bf16[2,2,4,2,64,192]{5,4,3,2,1,0:T(8,128)(2,1)} custom-call(bf16[4,2,4,64,192]{4,3,2,1,0:T(8,128)(2,1)} %bitcast.153), custom_call_target="tpu_custom_call" | custom-call | tf_op jit(solution)/shard_map/pallas_call | solution.py:535
  376.2 46.6 %shard_map.284 = bf16[2048,576]{1,0:T(8,128)(2,1)} custom-call(s32[1]{0:T(128)} %dynamic_slice.19.length, bf16[3,2048,64]{2,1,0:T(8,128)(2,1)} %get-tuple-element.49.query, bf16[3,2048,64]{2,1,0:T(8,128)(2,1)} %get-tuple-element.50.key, bf16[3,2048,64]{2,1,0:T(8,128)(2,1)} %get-tuple-element.51.value, bf16[2048,192]{1,0:T(8,128)(2,1)} %bitcast.151, ...), custom_call_target="tpu_custom_call" | custom-call | tf_op jit(solution)/shard_map/pallas_call | solution.py:822
  422.8 4.8 convolution_convert_fusion.4
  427.6 2.2 copy.53
  429.8 6.2 %convolution_convert_fusion.2 = bf16[2048,768]{1,0:T(8,128)(2,1)} fusion(bf16[2048,576]{1,0:T(8,128)(2,1)} %shard_map.284, bf16[768,576]{0,1:T(8,128)(2,1)} %bitcast.156), kind=kOutput, calls=%fused_computation.21 | convolution fusion | flops 1813512192 | bytes 6389760 | tf_op jit(solution)/shard_map/dot_general | solution.py:743
  436.0 32.9 %shard_map.285 = (f32[4,24,576]{2,1,0:T(8,128)}, f32[2,4,64,768]{3,2,1,0:T(8,128)}) custom-call(bf16[2,2,4,2,24,576]{5,4,3,2,1,0:T(8,128)(2,1)} %bitcast.154, bf16[2,2,4,2,64,768]{5,4,3,2,1,0:T(8,128)(2,1)} %bitcast.157), custom_call_target="tpu_custom_call" | custom-call | tf_op jit(solution)/shard_map/pallas_call | solution.py:535
  469.6 2.4 multiply_reduce_fusion
  472.0 3.0 fusion.12.grads
  475.1 0.5 convert_reduce_fusion.1
  476.3 0.7 pad.98.small
  477.0 26.7 %shard_map.286 = (bf16[8,64,768]{2,1,0:T(8,128)(2,1)}, f32[32,8,128]{2,1,0:T(8,128)}) custom-call(bf16[8,64,768]{2,1,0:T(8,128)(2,1)} %fusion.12.grads, f32[32,8,128]{2,1,0:T(8,128)} %pad.98.small), custom_call_target="tpu_custom_call" | custom-call | tf_op jit(solution)/shard_map/pallas_call | solution.py:535
  503.7 1.0 reduce_sum.208
  504.7 0.5 slice_bitcast_fusion.5
  505.6 0.9 reshape.562
  506.5 0.5 slice_bitcast_fusion
  507.0 0.5 slice_bitcast_fusion.1
  507.5 0.6 reduce_sum.209
  508.8 0.5 sqrt_bitcast_fusion
  509.3 0.9 copy.76
  510.2 0.9 copy.77
  511.1 0.6 copy.78
  511.7 0.7 copy.79
  512.5 0.7 copy.80
  (95 shorter events, 3.4 us)
Async XLA Ops:
  131.2 6.6 %copy-start.16 = (bf16[32,16,128]{2,1,0:T(8,128)(2,1)S(1)}, bf16[32,16,128]{2,1,0:T(8,128)(2,1)}, u32[]{:S(2)}) copy-start(bf16[32,16,128]{2,1,0:T(8,128)(2,1)} %get-tuple-element.41) | copy-start | bytes 393220
  140.4 63.9 %copy-start = (bf16[32,64,768]{2,1,0:T(8,128)(2,1)S(1)}, bf16[32,64,768]{2,1,0:T(8,128)(2,1)}, u32[]{:S(2)}) copy-start(bf16[32,64,768]{2,1,0:T(8,128)(2,1)} %get-tuple-element.39) | copy-start | bytes 9437188
  238.8 6.2 %copy-start.20 = (bf16[512,3072]{1,0:T(8,128)(2,1)}, bf16[512,3072]{1,0:T(8,128)(2,1)S(1)}, u32[]{:S(2)}) copy-start(bf16[512,3072]{1,0:T(8,128)(2,1)S(1)} %get-tuple-element.85) | copy-start | bytes 9437188
  238.8 6.2 %slice-start = ((s8[6291456]{0:T(1024)(128)(4,1)}), s8[4194304]{0:T(1024)(128)(4,1)S(1)}, s32[]{:S(2)}) async-start(s8[6291456]{0:T(1024)(128)(4,1)} %bitcast.147), calls=%async_computation | async-start | bytes 8388608
  238.8 6.2 %slice-start.1 = ((s8[6291456]{0:T(1024)(128)(4,1)}), s8[2097152]{0:T(1024)(128)(4,1)S(1)}, s32[]{:S(2)}) async-start(s8[6291456]{0:T(1024)(128)(4,1)} %bitcast.147), calls=%async_computation.1 | async-start | bytes 4194304
  245.0 3.3 copy-start.1
  248.3 8.6 %copy-start.3 = (bf16[8,64,768]{2,1,0:T(8,128)(2,1)S(1)}, bf16[8,64,768]{2,1,0:T(8,128)(2,1)}, u32[]{:S(2)}) copy-start(bf16[8,64,768]{2,1,0:T(8,128)(2,1)} %get-tuple-element.43) | copy-start | bytes 2359300
  256.9 1.8 copy-start.5
  258.7 1.8 copy-start.8
  258.7 2.6 copy-start.21
  261.3 4.8 copy-start.6
  274.0 82.7 %copy-start.7 = (bf16[32,24,768]{2,1,0:T(8,128)(2,1)S(1)}, bf16[32,24,768]{2,1,0:T(8,128)(2,1)}, u32[]{:S(2)}) copy-start(bf16[32,24,768]{2,1,0:T(8,128)(2,1)} %get-tuple-element.44) | copy-start | bytes 3538948
  274.0 82.7 %copy-start.9 = (bf16[512,768]{1,0:T(8,128)(2,1)S(1)}, bf16[512,768]{1,0:T(8,128)(2,1)}, u32[]{:S(2)}) copy-start(bf16[512,768]{1,0:T(8,128)(2,1)} %copy-done.8) | copy-start | bytes 2359300
  376.1 46.7 %copy-start.18 = (bf16[2048,768]{1,0:T(8,128)(2,1)S(1)}, bf16[2048,768]{1,0:T(8,128)(2,1)}, u32[]{:S(2)}) copy-start(bf16[2048,768]{1,0:T(8,128)(2,1)} %get-tuple-element.48) | copy-start | bytes 9437188
  469.6 2.4 copy-start.4
  472.0 3.0 copy-start.2
  475.0 30.2 %copy-start.14 = (f32[4,24,576]{2,1,0:T(8,128)S(1)}, f32[4,24,576]{2,1,0:T(8,128)}, u32[]{:S(2)}) copy-start(f32[4,24,576]{2,1,0:T(8,128)} %get-tuple-element.57) | copy-start | bytes 663556
  475.0 31.4 %copy-start.17 = (f32[8,128]{1,0:T(8,128)S(1)}, f32[8,128]{1,0:T(8,128)}, u32[]{:S(2)}) copy-start(f32[8,128]{1,0:T(8,128)} %get-tuple-element.59) | copy-start | bytes 12292
  475.1 32.5 %copy-start.19 = (s32[8]{0:T(128)S(1)}, s32[8]{0:T(128)}, u32[]{:S(2)}) copy-start(s32[8]{0:T(128)} %param.17) | copy-start | bytes 100
  475.1 34.3 %copy-start.10 = (bf16[8,64,768]{2,1,0:T(8,128)(2,1)S(1)}, bf16[8,64,768]{2,1,0:T(8,128)(2,1)}, u32[]{:S(2)}) copy-start(bf16[8,64,768]{2,1,0:T(8,128)(2,1)} %get-tuple-element.124) | copy-start | bytes 2359300
  476.3 34.8 %copy-start.15 = (f32[24,768]{1,0:T(8,128)S(1)}, f32[24,768]{1,0:T(8,128)}, u32[]{:S(2)}) copy-start(f32[24,768]{1,0:T(8,128)} %get-tuple-element.131) | copy-start | bytes 221188
  477.0 34.8 %copy-start.13 = (f32[24,3072]{1,0:T(8,128)S(1)}, f32[24,3072]{1,0:T(8,128)}, u32[]{:S(2)}) copy-start(f32[24,3072]{1,0:T(8,128)} %get-tuple-element.135) | copy-start | bytes 884740
  503.6 6.6 %copy-start.11 = (bf16[8,64,768]{2,1,0:T(8,128)(2,1)S(1)}, bf16[8,64,768]{2,1,0:T(8,128)(2,1)}, u32[]{:S(2)}) copy-start(bf16[8,64,768]{2,1,0:T(8,128)(2,1)} %get-tuple-element.125) | copy-start | bytes 2359300
  503.6 8.8 %copy-start.12 = (f32[96,768]{1,0:T(8,128)S(1)}, f32[96,768]{1,0:T(8,128)}, u32[]{:S(2)}) copy-start(f32[96,768]{1,0:T(8,128)} %get-tuple-element.137) | copy-start | bytes 884740

commit v2 on v1

--- a/solution.py
+++ b/solution.py
@@ -405,129 +405,310 @@
         self.send_sem = send_sem
         self.local_sem = local_sem
         self.anyone = anyone
+        self.zero = anyone[0] * 0
         self.sent = []
         self.local = []
 
     def push(self, source, target, sem, device):
-        copy = pltpu.make_async_remote_copy(
-            src_ref=source,
-            dst_ref=target,
-            send_sem=self.send_sem.at[len(self.sent)],
-            recv_sem=sem,
-            device_id=device,
-            device_id_type=MESH,
-        )
-        copy.start()
-        self.sent.append(copy)
+        self.sent.append((source, target, len(self.sent), sem, device))
+        self.start(*self.sent[-1])
+
+    def start(self, source, target, spot, sem, device):
+        sem = sem[0].at[self.zero + sem[1], sem[2]] if isinstance(sem, tuple) else sem
+        remote(source, target, self.send_sem.at[self.zero + spot], sem, device).start()
+
+    def sent_off(self, source, target, spot, sem, device):
+        sem = sem[0].at[self.zero + sem[1], sem[2]] if isinstance(sem, tuple) else sem
+        remote(source, target, self.send_sem.at[self.zero + spot], sem, device).wait_send()
 
     def keep(self, source, target):
-        copy = pltpu.make_async_copy(source, target, self.local_sem.at[len(self.local)])
-        copy.start()
-        self.local.append(copy)
-        return copy
+        parts = (source, target, self.local_sem.at[len(self.local)])
+        pltpu.make_async_copy(*parts).start()
+        self.local.append(parts)
 
     def landed(self, target, sem):
-        pltpu.make_async_remote_copy(
-            src_ref=target,
-            dst_ref=target,
-            send_sem=self.send_sem.at[0],
-            recv_sem=sem,
-            device_id=self.anyone,
-            device_id_type=MESH,
-        ).wait_recv()
+        remote(target, target, self.send_sem.at[self.zero], sem, self.anyone).wait_recv()
 
     def finish(self):
-        for copy in self.sent:
-            copy.wait_send()
-        for copy in self.local:
-            copy.wait()
-
-
-def spread_kernel(
-    tokens, cotangent, wj, wo, wi, wu, small,
-    tok_all, cot_own, wj_all, wo_all, wi_all, wu_all, small_all,
-    send_sem, local_sem, tok_sem, cot_sem, weight_sem,
+        for parts in self.sent:
+            self.sent_off(*parts)
+        for parts in self.local:
+            pltpu.make_async_copy(*parts).wait()
+
+
+def remote(source, target, send_sem, recv_sem, device):
+    return pltpu.make_async_remote_copy(
+        src_ref=source,
+        dst_ref=target,
+        send_sem=send_sem,
+        recv_sem=recv_sem,
+        device_id=device,
+        device_id_type=MESH,
+    )
+
+
+def unpack(small_all, vectors):
+    for block in range(32):
+        tile = wide(small_all[block])
+        vectors[:, block * 24 : block * 24 + 24] = tile[:8, :24]
+
+
+def forward_kernel(
+    length, tokens, cotangent, wj, wo, wi, wu, small,
+    first_low, query, key, value, context, context_rows, cot_own, tok_own, wo_all, wi_all, wu_all, small_all, wj_flat,
+    send_sem, local_sem, tok_sem, cot_sem, weight_sem, small_sem, wja_sem, wjb_sem, wjc_sem, ctx_send, ctx_recv,
+    ctx_local, tok_all, wj_all, vectors, turned, mixed_low,
 ):
     y, x, z, c = place()
     mine = number(y, x, z, c)
+    quarter = x * 2 + c
     spot = y * 4 + z
     other_core = at(y, x, z, 1 - c)
     across = at(y, 1 - x, z, c)
+    diagonal = at(y, 1 - x, z, 1 - c)
+    down = at(1 - y, x, z, c)
     y1, x1 = jnp.where(c == 0, y, 1 - y), jnp.where(c == 0, 1 - x, x)
     y2, x2 = jnp.where(c == 0, 1 - y, y), jnp.where(c == 0, x, 1 - x)
     first, second = at(y1, x1, z, c), at(y2, x2, z, c)
     spots = [column(lax.rem(spot + k, 8)) for k in range(1, 8)]
-    peers = [at(yy, x, zz, c) for yy, zz in spots] + [across, other_core]
-    meet(peers)
+    back_spots = [column(lax.rem(spot + 8 - k, 8)) for k in range(1, 8)]
+    lines = [lax.rem(z + 4 - k, 4) for k in range(4)]
+    ahead = [at(y, x, lax.rem(z + k, 4), c) for k in range(1, 4)]
+    line_blocks = [number(y, x, zz, c) for zz in lines]
+    first_blocks = [number(y1, x1, zz, c) for zz in lines]
+    second_blocks = [number(yy, xx, zz, c) for yy, xx in ((y2, x2), (1 - y, 1 - x)) for zz in lines]
+    core_blocks = [number(yy, xx, zz, 1 - c) for yy in range(2) for xx in range(2) for zz in range(4)]
+    group = quad(x, c)
+    meet([at(yy, x, zz, c) for yy, zz in spots] + [across, other_core, diagonal])
     move = Mover(send_sem, local_sem, other_core)
-    sources = (wj, wo, wi, wu, small)
-    wholes = (wj_all, wo_all, wi_all, wu_all, small_all)
+    sources = (wo, wi, wu)
+    wholes = (wo_all, wi_all, wu_all)
 
     for yy, zz in spots:
         move.push(tokens.at[yy * 4 + zz], tok_all.at[mine], tok_sem.at[mine], at(yy, x, zz, c))
+    for xx, cc in group:
+        move.push(wj.at[xx * 2 + cc], wj_all.at[y, x, z, c], wja_sem.at[quarter], at(y, xx, z, cc))
+    move.keep(wj.at[quarter], wj_all.at[y, x, z, c])
     move.push(tokens.at[spot], tok_all.at[mine], tok_sem.at[mine], across)
     move.push(tokens.at[spot], tok_all.at[mine], tok_sem.at[mine], other_core)
     move.keep(tokens.at[spot], tok_all.at[mine])
+    for device in ahead + [first, second, other_core]:
+        move.push(small, small_all.at[mine], small_sem.at[mine], device)
+    move.keep(small, small_all.at[mine])
 
     def hand(block, own, device):
-        for i, (source, whole) in enumerate(zip(sources, wholes)):
+        for i in range(3):
             move.push(
-                source if own else whole.at[block], whole.at[block], weight_sem.at[i, block], device
+                sources[i] if own else wholes[i].at[block],
+                wholes[i].at[block],
+                (weight_sem, i, block),
+                device,
             )
 
     def arrive(block):
-        for i, whole in enumerate(wholes):
-            move.landed(whole.at[block], weight_sem.at[i, block])
-
-    for k in range(1, 4):
-        hand(mine, True, at(y, x, lax.rem(z + k, 4), c))
+        for i in range(3):
+            move.landed(wholes[i].at[block], weight_sem.at[i, block])
+
+    def pass_small(blocks, devices):
+        for block in blocks:
+            move.landed(small_all.at[block], small_sem.at[block])
+            for device in devices:
+                move.push(small_all.at[block], small_all.at[block], small_sem.at[block], device)
+
+    for device in ahead:
+        hand(mine, True, device)
     for source, whole in zip(sources, wholes):
         move.keep(source, whole.at[mine])
     hand(mine, True, first)
     hand(mine, True, second)
     hand(mine, True, other_core)
-    for yy, zz in spots:
-        move.push(cotangent.at[yy * 4 + zz], cot_own.at[spot], cot_sem.at[spot], at(yy, x, zz, c))
-    move.keep(cotangent.at[spot], cot_own.at[spot])
-
-    back_spots = [column(lax.rem(spot + 8 - k, 8)) for k in range(1, 8)]
+
+    for xx, cc in group:
+        move.landed(wj_all.at[y, xx, z, cc], wja_sem.at[xx * 2 + cc])
+    pltpu.make_async_copy(*move.local[0]).wait()
+    for device in ahead:
+        move.push(wj_all.at[y, :, z], wj_all.at[y, :, z], wjb_sem.at[z], device)
+    move.push(wj_all.at[y, :, z], wj_all.at[y, :, z], wjc_sem.at[z], down)
+    pass_small(line_blocks[1:], (first, second, other_core))
     for yy, zz in back_spots:
         block = number(yy, x, zz, c)
         move.landed(tok_all.at[block], tok_sem.at[block])
         move.push(tok_all.at[block], tok_all.at[block], tok_sem.at[block], across)
         move.push(tok_all.at[block], tok_all.at[block], tok_sem.at[block], other_core)
-    lines = [lax.rem(z + 4 - k, 4) for k in range(4)]
     for zz in lines[1:]:
-        block = number(y, x, zz, c)
+        move.landed(wj_all.at[y, :, zz], wjb_sem.at[zz])
+        move.push(wj_all.at[y, :, zz], wj_all.at[y, :, zz], wjc_sem.at[zz], down)
+    for yy, zz in spots:
+        move.push(cotangent.at[yy * 4 + zz], cot_own.at[spot], cot_sem.at[spot], at(yy, x, zz, c))
+    move.keep(cotangent.at[spot], cot_own.at[spot])
+    pass_small(first_blocks, (second, other_core))
+    pass_small(second_blocks, (other_core,))
+    for yy, zz in [(y, z)] + back_spots:
+        block = number(yy, 1 - x, zz, c)
+        move.landed(tok_all.at[block], tok_sem.at[block])
+        move.push(tok_all.at[block], tok_all.at[block], tok_sem.at[block], other_core)
+    for block in line_blocks[1:]:
         arrive(block)
         hand(block, False, first)
         hand(block, False, second)
         hand(block, False, other_core)
-    for yy, zz in [(y, z)] + back_spots:
-        block = number(yy, 1 - x, zz, c)
-        move.landed(tok_all.at[block], tok_sem.at[block])
-        move.push(tok_all.at[block], tok_all.at[block], tok_sem.at[block], other_core)
+    for block in core_blocks:
+        move.landed(small_all.at[block], small_sem.at[block])
     for zz in lines:
-        block = number(y1, x1, zz, c)
-        arrive(block)
-        hand(block, False, second)
-        hand(block, False, other_core)
-    for yy, xx in ((y2, x2), (1 - y, 1 - x)):
-        for zz in lines:
-            block = number(yy, xx, zz, c)
-            arrive(block)
-            hand(block, False, other_core)
+        move.landed(wj_all.at[1 - y, :, zz], wjc_sem.at[zz])
     for yy, zz in [(y, z)] + back_spots:
         for xx in (x, 1 - x):
             block = number(yy, xx, zz, 1 - c)
             move.landed(tok_all.at[block], tok_sem.at[block])
-    for yy, zz in back_spots:
-        move.landed(cot_own.at[yy * 4 + zz], cot_sem.at[yy * 4 + zz])
+    for parts in move.local[1:3]:
+        pltpu.make_async_copy(*parts).wait()
+
+    unpack(small_all, vectors)
+    rows = query.shape[1]
     for yy in range(2):
         for xx in range(2):
             for zz in range(4):
-                arrive(number(yy, xx, zz, 1 - c))
-    move.finish()
+                pair = jnp.concatenate([wide(wj_all[yy, xx, zz, cc]) for cc in range(2)], axis=0)
+                row = number(yy, xx, zz, 0) * 24
+                wj_flat[row : row + 48, :] = pair.astype(jnp.bfloat16)
+    lane = lax.broadcasted_iota(jnp.int32, (ROWS, DH), 1)
+    row_at = lax.broadcasted_iota(jnp.int32, (ROWS, DH), 0)
+    one_lane = jnp.where(lane == 0, 1.0, 0.0).astype(jnp.bfloat16)
+    three_lanes = jnp.where(lane < 3, 1.0, 0.0).astype(jnp.bfloat16)
+    gain, shift = vectors[0:1, :], vectors[1:2, :]
+    query_all, value_all = vectors[2:3, :], vectors[3:4, :]
+
+    def chosen(whole):
+        total = jnp.zeros((1, GROUP), jnp.float32)
+        for q in range(4):
+            total = jnp.where(quarter == q, whole[:, q * GROUP : (q + 1) * GROUP], total)
+        return total
+
+    query_shift, value_shift = chosen(query_all), chosen(value_all)
+    blocks = ROWS // tokens.shape[1]
+
+    def project(i, _):
+        here = pl.ds(i * ROWS, ROWS)
+        raw = tok_all[pl.ds(i * blocks, blocks)].reshape(ROWS, WIDTH)
+        normed = normalize(wide(raw), gain, shift)[0].astype(jnp.bfloat16)
+        first_low[here, :] = normed
+        joint = dot(normed, wj_flat[...])
+        low_q = ((joint[:, :GROUP] + query_shift).astype(jnp.bfloat16) * DH ** (-0.5)).astype(jnp.bfloat16)
+        low_k = joint[:, GROUP : 2 * GROUP].astype(jnp.bfloat16)
+        low_v = (joint[:, 2 * GROUP :] + value_shift).astype(jnp.bfloat16)
+        mask = jnp.where(row_at + i * ROWS < length[0], 0.0, NEG)
+        key_side = jnp.where(lane == 0, mask, jnp.where(lane < 4, 1.0, 0.0)).astype(jnp.bfloat16)
+        for h in range(3):
+            here_h = slice(h * DH, (h + 1) * DH)
+            query[h, here, :] = jnp.concatenate([low_q[:, here_h], one_lane], axis=1)
+            key[h, here, :] = jnp.concatenate([low_k[:, here_h], key_side], axis=1)
+            value[h, here, :] = jnp.concatenate([low_v[:, here_h], three_lanes], axis=1)
+        return 0
+
+    lax.fori_loop(0, rows // ROWS, project, 0)
+    eye = jnp.eye(72, 2 * DH, dtype=jnp.bfloat16)
+    for h in range(3):
+        turned[h] = dot(eye, value[h], NT).astype(jnp.bfloat16)
+    side = lax.broadcasted_iota(jnp.int32, (DH, ROWS), 0)
+
+    def ctx_piece(j, cc):
+        yy, xx, zz = j // 4, lax.rem(j // 2, 2), pl.ds(lax.rem(j, 2) * 2, 2)
+        return mixed_low.at[yy, xx, zz, cc], context_rows.at[quarter, yy, zz]
+
+    def block(j, _):
+        here = pl.ds(j * ROWS, ROWS)
+        whole = []
+        for h in range(3):
+            scores = dot(key[h], query[h, here, :], NT)
+            best = jnp.max(scores, axis=0, keepdims=True)
+            weights = jnp.exp(scores - best).astype(jnp.bfloat16)
+            mixed = dot(turned[h], weights)
+            total = mixed[DH : DH + 1, :]
+            mixed = mixed[:DH, :] / total
+            log_total = best + jnp.log(total)
+            high = log_total.astype(jnp.bfloat16).astype(jnp.float32)
+            middle = (log_total - high).astype(jnp.bfloat16).astype(jnp.float32)
+            low = log_total - high - middle
+            extra = jnp.where(
+                side == 0, 1.0, jnp.where(side == 1, -high, jnp.where(side == 2, -middle, jnp.where(side == 3, -low, 0.0)))
+            )
+            straight = jnp.concatenate([mixed, extra], axis=0).T
+            query[h, here, DH:] = straight[:, DH:].astype(jnp.bfloat16)
+            whole.append(straight[:, :DH])
+        mixed = jnp.concatenate(whole, axis=1)
+        context[here, :] = mixed
+        yy, xx, zz = j // 4, lax.rem(j // 2, 2), lax.rem(j, 2) * 2
+        low = mixed.astype(jnp.bfloat16)
+        piece = tokens.shape[1]
+        for k in range(2):
+            for cc in range(2):
+                start = (k * 2 + cc) * piece
+                mixed_low[yy, xx, zz + k, cc] = low[start : start + piece]
+        for cc in range(2):
+            source, target = ctx_piece(j, cc)
+
+            @pl.when(jnp.logical_and(xx == x, c == cc))
+            def _():
+                pltpu.make_async_copy(source, target, ctx_local.at[j]).start()
+
+            @pl.when(jnp.logical_not(jnp.logical_and(xx == x, c == cc)))
+            def _():
+                remote(source, target, ctx_send.at[j, cc], ctx_recv.at[quarter, j], at(y, xx, z, cc)).start()
+
+        @pl.when(j == 2)
+        def _():
+            for b in first_blocks:
+                arrive(b)
+                hand(b, False, second)
+                hand(b, False, other_core)
+
+        @pl.when(j == 6)
+        def _():
+            for b in second_blocks:
+                arrive(b)
+                hand(b, False, other_core)
+
+        return 0
+
+    lax.fori_loop(0, rows // ROWS, block, 0)
+    for yy, zz in back_spots:
+        move.landed(cot_own.at[yy * 4 + zz], cot_sem.at[yy * 4 + zz])
+    for b in core_blocks:
+        arrive(b)
+    tok_copies = []
+    for i in range(8):
+        yy, zz = i // 4, i % 4
+        tok_copies.append(pltpu.make_async_copy(tok_all.at[number(yy, x, zz, c)], tok_own.at[i], local_sem.at[8 + i]))
+        tok_copies[-1].start()
+
+    def settle(j, _):
+        xx = lax.rem(j // 2, 2)
+        for cc in range(2):
+            source, target = ctx_piece(j, cc)
+
+            @pl.when(jnp.logical_and(xx == x, c == cc))
+            def _():
+                pltpu.make_async_copy(source, target, ctx_local.at[j]).wait()
+
+            @pl.when(jnp.logical_not(jnp.logical_and(xx == x, c == cc)))
+            def _():
+                remote(source, target, ctx_send.at[j, cc], ctx_recv.at[quarter, j], at(y, xx, z, cc)).wait_send()
+
+        return 0
+
+    lax.fori_loop(0, rows // ROWS, settle, 0)
+    for xx, cc in group:
+        for yy in range(2):
+            for half in range(2):
+                j = yy * 4 + x * 2 + half
+                target = context_rows.at[xx * 2 + cc, yy, pl.ds(half * 2, 2)]
+                move.landed(target, ctx_recv.at[xx * 2 + cc, j])
+    for parts in move.sent:
+        move.sent_off(*parts)
+    for parts in move.local[3:]:
+        pltpu.make_async_copy(*parts).wait()
+    for copy in tok_copies:
+        copy.wait()
 
 
 def comm_call(kernel, outs, args, sends, locals_, sems, scratch, ident, space=None):
@@ -551,24 +732,6 @@
 
 def quad(x, c):
     return [(lax.rem(x + dx, 2), lax.rem(c + dc, 2)) for dx, dc in ((0, 1), (1, 0), (1, 1))]
-
-
-def to_rows_kernel(source, target, send_sem, local_sem, recv_sem):
-    y, x, z, c = place()
-    mine = x * 2 + c
-    meet([at(y, xx, z, cc) for xx, cc in quad(x, c)])
-    move = Mover(send_sem, local_sem, at(y, x, z, 1 - c))
-    for xx, cc in quad(x, c)[::-1]:
-        for yy in range(2):
-            move.push(
-                source.at[yy, xx, :, cc], target.at[mine, yy], recv_sem.at[mine, yy], at(y, xx, z, cc)
-            )
-    for yy in range(2):
-        move.keep(source.at[yy, x, :, c], target.at[mine, yy])
-    for xx, cc in quad(x, c):
-        for yy in range(2):
-            move.landed(target.at[xx * 2 + cc, yy], recv_sem.at[xx * 2 + cc, yy])
-    move.finish()
 
 
 def to_heads_kernel(source, target, send_sem, local_sem, recv_sem):
@@ -746,54 +909,11 @@
 ROWS = 256
 
 
-def attend_kernel(
-    length, tok, wj, gain, shift, query_shift, value_shift, first, query, key, value, context, context_turned, log_total
-):
-    rows = tok.shape[0]
-
-    def project(i, _):
-        here = pl.ds(i * ROWS, ROWS)
-        normed = normalize(wide(tok[here, :]), gain[...], shift[...])[0].astype(jnp.bfloat16)
-        first[here, :] = normed
-        joint = dot(normed, wj[...])
-        low_q = (joint[:, :GROUP] + query_shift[...]).astype(jnp.bfloat16)
-        low_k = joint[:, GROUP : 2 * GROUP].astype(jnp.bfloat16)
-        low_v = (joint[:, 2 * GROUP :] + value_shift[...]).astype(jnp.bfloat16)
-        for h in range(3):
-            query[h, here, :] = low_q[:, h * DH : (h + 1) * DH]
-            key[h, here, :] = low_k[:, h * DH : (h + 1) * DH]
-            value[h, here, :] = low_v[:, h * DH : (h + 1) * DH]
-        return 0
-
-    lax.fori_loop(0, rows // ROWS, project, 0)
-    keep = lax.broadcasted_iota(jnp.int32, (rows, 1), 0) < length[0]
-    eye = jnp.eye(DH, dtype=jnp.bfloat16)
-    for h in range(3):
-        turned = dot(eye, value[h], NT).astype(jnp.bfloat16)
-
-        def block(i, _):
-            here = pl.ds(i * ROWS, ROWS)
-            scores = dot(key[h], query[h, here, :], NT) * DH ** (-0.5)
-            scores = jnp.where(keep, scores, NEG)
-            best = jnp.max(scores, axis=0, keepdims=True)
-            weights = jnp.exp(scores - best)
-            total = jnp.sum(weights, axis=0, keepdims=True)
-            mixed = dot(turned, weights.astype(jnp.bfloat16)) / total
-            context_turned[h, :, here] = mixed
-            log_total[h, :, here] = best + jnp.log(total)
-            context[here, h * DH : (h + 1) * DH] = mixed.T.astype(jnp.bfloat16)
-            return 0
-
-        lax.fori_loop(0, rows // ROWS, block, 0)
-
-
-def attend_back_kernel(
-    length, query, key, value, back_context, context_turned, log_total, joint, key_sum, value_sum
-):
+def attend_back_kernel(query, key, value, back_context, context, joint, key_sum, value_sum):
     rows = query.shape[1]
     scale = DH ** (-0.5)
-    keep = lax.broadcasted_iota(jnp.int32, (rows, 1), 0) < length[0]
-    eye = jnp.eye(DH, dtype=jnp.bfloat16)
+    eye = jnp.eye(DH, 2 * DH, dtype=jnp.bfloat16)
+    lane = lax.broadcasted_iota(jnp.int32, (ROWS, DH), 1)
     for h in range(3):
         turned = dot(eye, key[h], NT).astype(jnp.bfloat16)
         key_sum[...] = jnp.zeros_like(key_sum)
@@ -803,18 +923,21 @@
             here = pl.ds(i * ROWS, ROWS)
             queries = query[h, here, :]
             backs = back_context[here, h * DH : (h + 1) * DH]
-            scores = dot(key[h], queries, NT) * scale
-            scores = jnp.where(keep, scores, NEG)
-            chances = jnp.exp(scores - log_total[h, :, here])
-            spread = jnp.sum(dot(eye, backs, NT) * context_turned[h, :, here], axis=0, keepdims=True)
-            back_scores = (chances * (dot(value[h], backs, NT) - spread)).astype(jnp.bfloat16)
+            spread = jnp.sum(wide(backs) * context[here, h * DH : (h + 1) * DH], axis=1, keepdims=True)
+            high = spread.astype(jnp.bfloat16).astype(jnp.float32)
+            middle = (spread - high).astype(jnp.bfloat16).astype(jnp.float32)
+            low = spread - high - middle
+            side = jnp.where(lane == 0, -high, jnp.where(lane == 1, -middle, jnp.where(lane == 2, -low, 0.0)))
+            widened = jnp.concatenate([backs, side.astype(jnp.bfloat16)], axis=1)
+            chances = jnp.exp(dot(key[h], queries, NT))
+            back_scores = (chances * dot(value[h], widened, NT)).astype(jnp.bfloat16)
             joint[here, h * DH : (h + 1) * DH] = (dot(turned, back_scores) * scale).T.astype(jnp.bfloat16)
-            key_sum[...] += dot(back_scores, queries)
+            key_sum[...] += dot(back_scores, queries[:, :DH])
             value_sum[...] += dot(chances.astype(jnp.bfloat16), backs)
             return 0
 
         lax.fori_loop(0, rows // ROWS, block, 0)
-        joint[:, GROUP + h * DH : GROUP + (h + 1) * DH] = (key_sum[...] * scale).astype(jnp.bfloat16)
+        joint[:, GROUP + h * DH : GROUP + (h + 1) * DH] = key_sum[...].astype(jnp.bfloat16)
         joint[:, 2 * GROUP + h * DH : 2 * GROUP + (h + 1) * DH] = value_sum[...].astype(jnp.bfloat16)
 
 
@@ -859,72 +982,71 @@
     mine = x * 2 + c
     slots, piece, width = tokens.shape
     ff = inner_weight.shape[1]
-    small = packed(
-        [first_gain, first_bias, query_bias, value_bias, output_bias, second_gain, second_bias, outer_bias, inner_bias],
-        1, bf16, 16,
-    )[0]
+    short = jnp.stack(
+        [first_gain, first_bias, query_bias, value_bias, output_bias, second_gain, second_bias, outer_bias]
+    )
+    lead = short.shape[1]
+    ff_piece = inner_bias.shape[0]
+    small = jnp.concatenate(
+        [
+            jnp.pad(short, ((0, 0), (0, ff_piece - lead))),
+            jnp.broadcast_to(inner_bias, (8, ff_piece)),
+        ],
+        axis=0,
+    )
     hbm, vmem = pltpu.HBM, pltpu.VMEM
-    tok_all, cot_own, wj_all, wo_all, wi_all, wu_all, small_all = comm_call(
-        spread_kernel,
+    dma, regular = pltpu.SemaphoreType.DMA, pltpu.SemaphoreType.REGULAR
+    rows_all = 32 * piece
+    natural = (2, 2, 4, 2, piece)
+    length = lax.dynamic_slice(lengths, (y * 4 + z,), (1,))
+    joint_four = jnp.transpose(joint_weight.reshape(lead, 3, 4, GROUP), (2, 0, 1, 3)).reshape(4, lead, 3 * GROUP)
+    forward_outs = [
+        ((rows_all, width), bf16, vmem),
+        ((3, rows_all, 2 * DH), bf16, vmem),
+        ((3, rows_all, 2 * DH), bf16, vmem),
+        ((3, rows_all, 2 * DH), bf16, vmem),
+        ((rows_all, GROUP), f32, vmem),
+        ((4, 2, 4, piece, GROUP), bf16, vmem),
+        ((8, piece, width), bf16, hbm),
+        ((8, piece, width), bf16, hbm),
+        ((32,) + output_weight.shape, bf16, hbm),
+        ((32,) + inner_weight.shape, bf16, hbm),
+        ((32,) + outer_weight.shape, bf16, hbm),
+        ((32,) + small.shape, bf16, vmem),
+        ((width, 3 * GROUP), bf16, vmem),
+    ]
+    (
+        first_low, query, key, value, context, context_rows, cot_own, tok_own, wo_all, wi_all, wu_all, small_all, joint_here
+    ) = comm_call(
+        forward_kernel,
+        forward_outs,
+        (length, tokens, cotangent, joint_four, output_weight, inner_weight, outer_weight, small),
+        220, 16,
+        [(32,), (8,), (3, 32), (32,), (4,), (4,), (4,), (8, 2), (4, 8), (8,)],
         [
-            ((32, piece, width), bf16, hbm),
-            ((8, piece, width), bf16, hbm),
-            ((32,) + joint_weight.shape, bf16, hbm),
-            ((32,) + output_weight.shape, bf16, hbm),
-            ((32,) + inner_weight.shape, bf16, hbm),
-            ((32,) + outer_weight.shape, bf16, hbm),
-            ((32, 16, 128), bf16, hbm),
+            vmem((32, piece, width), bf16),
+            vmem((2, 2, 4, 2, lead, 3 * GROUP), bf16),
+            vmem((8, width), f32),
+            vmem((3, 72, rows_all), bf16),
+            vmem(natural + (GROUP,), bf16),
         ],
-        (tokens, cotangent, joint_weight, output_weight, inner_weight, outer_weight, small),
-        200, 8, [(32,), (8,), (5, 32)], [], 0,
-    )
-    vectors = jnp.transpose(small_all[:, :8, :24], (1, 0, 2)).reshape(8, width).astype(f32)
-    inner_shift = small_all[:, 8, :96].reshape(1, ff).astype(f32)
+        0,
+        [pltpu.SMEM, hbm, hbm, hbm, hbm, hbm, hbm, hbm],
+    )
+    vectors = jnp.transpose(small_all[:, :8, :lead], (1, 0, 2)).reshape(8, width).astype(f32)
+    inner_shift = small_all[:, 8, :ff_piece].reshape(1, ff).astype(f32)
     gain_one, shift_one, query_shift, value_shift, output_shift, gain_two, shift_two, outer_shift = (
         vectors[i : i + 1] for i in range(8)
     )
-    length = lax.dynamic_slice(lengths, (y * 4 + z,), (1,))
-    joint_full = wj_all.reshape(width, 3, 4, GROUP)
-    joint_here = lax.dynamic_index_in_dim(joint_full, mine, 2, keepdims=False).reshape(width, 3 * GROUP)
-    rows_all = 32 * piece
-    tok_flat = tok_all.reshape(rows_all, width)
-    first_low, query, key, value, context, context_turned, log_total = local_call(
-        attend_kernel,
-        [
-            ((rows_all, width), bf16),
-            ((3, rows_all, DH), bf16),
-            ((3, rows_all, DH), bf16),
-            ((3, rows_all, DH), bf16),
-            ((rows_all, GROUP), bf16),
-            ((3, DH, rows_all), f32),
-            ((3, 1, rows_all), f32),
-        ],
-        (
-            length, tok_flat, joint_here, gain_one, shift_one,
-            lax.dynamic_slice(query_shift, (0, mine * GROUP), (1, GROUP)),
-            lax.dynamic_slice(value_shift, (0, mine * GROUP), (1, GROUP)),
-        ),
-    )
-    natural = (2, 2, 4, 2, piece)
-    (context_rows,) = comm_call(
-        to_rows_kernel,
-        [((4, 2, 4, piece, GROUP), bf16, hbm)],
-        (context.reshape(natural + (GROUP,)),),
-        6, 2, [(4, 2)], [], 1,
-    )
     rows = 8 * piece
     context_low = jnp.transpose(context_rows.reshape(4, rows, GROUP), (1, 0, 2)).reshape(rows, width)
-
-    def own_rows(whole):
-        whole = lax.dynamic_index_in_dim(whole.reshape(natural + (-1,)), x, 1, keepdims=False)
-        return lax.dynamic_index_in_dim(whole, c, 2, keepdims=False).reshape(rows, -1)
 
     spots = jnp.arange(8, dtype=jnp.int32)
     position = (
         number(spots // 4, x, spots % 4, c)[:, None] * piece + jnp.arange(piece, dtype=jnp.int32)
     ).reshape(rows, 1)
     keep = position < length[0]
-    inputs = own_rows(tok_all).astype(f32)
+    inputs = tok_own.reshape(rows, width).astype(f32)
     output_full = wo_all.reshape(width, width)
     inner_full = wi_all.reshape(width, ff)
     outer_full = wu_all.reshape(ff, width)
@@ -967,8 +1089,9 @@
     (back_joint,) = local_call(
         attend_back_kernel,
         [((rows_all, 3 * GROUP), bf16)],
-        (length, query, key, value, back_heads.reshape(rows_all, GROUP), context_turned, log_total),
+        (query, key, value, back_heads.reshape(rows_all, GROUP), context),
         scratch=[vmem((rows_all, DH), f32), vmem((rows_all, DH), f32)],
+        smem=0,
     )
     stat_row = jnp.broadcast_to(jnp.stack(sums), (32, 3)).reshape(-1)
     small_one = packed(
@@ -998,7 +1121,6 @@
     )
     joint_gradient = dot(first_low, back_joint, turn).astype(bf16)
     back_first_part = dot(back_joint, joint_here, NT).astype(bf16)
-    lead = joint_weight.shape[0]
     joint_parts, back_first = comm_call(
         last_kernel,
         [((4, lead, 3 * GROUP), f32, vmem), ((2, 4, piece, width), f32, vmem)],

time: 517 us -> 449 us (0.87); the launches traced: 513 us -> 440 us
  Pallas kernels: 372 us -> 332 us
  local copies, waits for them, and re-layouts: 49.5 us -> 21.5 us
    pallas_call x2 -> x1, Pallas kernels: 91.3 us -> 46.1 us  [local_call(): pl.pallas_call(kernel, out_shape=[jax.ShapeDtypeStruct(shape, dtype) for...]
    reshape x2 -> x3, local copies, waits for them, and re-layouts: 12.4 us -> 1.96 us  [the longest x2 1.14 us: owner_device(): joint_weight.reshape(lead, 3, 4, GROUP)]
    dynamic_slice x3 -> x0, local copies, waits for them, and re-layouts: 9.78 us -> none  [the longest x2 9.14 us: owner_device(): lax.dynamic_index_in_dim(joint_full, mine, 2, keepdims=False)]
    pad x9 -> x0, local copies, waits for them, and re-layouts: 5.95 us -> none  [packed(): jnp.pad(v.reshape(blocks, 1, -1), ((0, 0), (0, 0), (0, 128 - v.size // bl...]
    pallas_call x6 -> x5, Pallas kernels: 281 us -> 286 us  [comm_call(): pl.pallas_call(kernel, out_shape=[jax.ShapeDtypeStruct(shape, dtype) for...]
where the time goes in v2:
time: 449 us; the launch traced here: 440 us
  Pallas kernels  332 us (74%)
  matrix products  66.6 us (15%)
  local copies, waits for them, and re-layouts  21.5 us (5%)
  other arithmetic  17.5 us (4%)
    pallas_call x5, Pallas kernels, comm_call(): pl.pallas_call(kernel, out_shape=[jax.ShapeDtypeStruct(shape, dtype) for...  286 us
    dot_general x10, matrix products, dot(): return lax.dot_general(a, b, dims, preferred_element_type=jnp.float32)  65.8 us
    pallas_call x1, Pallas kernels, local_call(): pl.pallas_call(kernel, out_shape=[jax.ShapeDtypeStruct(shape, dtype) for...  46.1 us

profile of v2, /device:TPU:0, one launch (start us, length us, event | category | flops | bytes accessed | tf_op | source)
XLA Modules:
  0.0 440.0 jit_solution(13902637991523700325)
XLA Ops:
  0.7 1.2 dynamic_slice.3.length
  1.9 1.1 reshape.470
  3.1 0.8 reshape.471.wj
  3.9 0.8 stack.47
  4.7 0.7 broadcast_in_dim.56
  5.3 0.6 fusion.18.small
  5.9 130.6 %shard_map.279 = (bf16[2048,768]{1,0:T(8,128)(2,1)}, bf16[3,2048,128]{2,1,0:T(8,128)(2,1)}, bf16[3,2048,128]{2,1,0:T(8,128)(2,1)}, bf16[3,2048,128]{2,1,0:T(8,12...) custom-call(s32[1]{0:T(128)} %dynamic_slice.3.length, ...), custom_call_target="tpu_custom_call" | custom-call | tf_op jit(solution)/shard_map/pallas_call | solution.py:716
  136.6 1.5 copy.46
  138.1 0.8 add_compare_fusion
  138.8 0.1 lt.32
  138.9 0.8 convert_bitcast_fusion
  139.8 0.2 slice_reduce_fusion
  140.1 3.6 fusion.28
  143.8 0.1 mul.216
  143.9 0.3 multiply_reduce_fusion.5
  144.3 7.2 %fusion.25 = f32[512,3072]{1,0:T(8,128)} fusion(bf16[768,3072]{1,0:T(8,128)(2,1)} %bitcast.152, f32[512,768]{1,0:T(8,128)S(1)} %get-tuple-element.88, f32[768]{0:T(1024)S(1)} %add.206, f32[768]{0:T(1024)S(1)} %mul.216, f32[512]{0:T(512)S(1)} %add_rsqrt_fusion.1, f32[512]{0:T(512)S(1)} %broadcast_multiply_fusion.5), kind=kOutput, calls=%fused_computation.123 | convolution fusion | flops 2417885184 | bytes 12593152 | tf_op jit(solution)/shard_map/dot_general | solution.py:906
  151.4 0.9 convert_reduce_fusion.5
  152.4 0.2 convert_reduce_fusion.4
  152.6 0.5 convert_reduce_fusion.3
  153.2 18.7 %convert_reduce_fusion = (f32[3072]{0:T(1024)S(1)}, bf16[512,3072]{1,0:T(8,128)(2,1)S(1)}, f32[512,3072]{1,0:T(8,128)S(1)}) fusion(f32[512,3072]{1,0:T(8,128)} %fusion.25, f32[3072]{0:T(1024)S(1)} %reshape.500, bf16[512,768]{1,0:T(8,128)(2,1)S(1)} %bitcast.132, bf16[3072,768]{1,0:T(8,128)(2,1)} %bitcast.150), kind=kOutput, calls=%fused_computation.2 | convolution fusion | flops 2533880832 | bytes 21258240 | tf_op jit(solution)/shard_map/dot_general | solution.py:906
  171.9 7.3 %fusion.29 = f32[512,768]{1,0:T(8,128)} fusion(bf16[512,3072]{1,0:T(8,128)(2,1)S(1)} %get-tuple-element.80, bf16[768,3072]{1,0:T(8,128)(2,1)} %bitcast.153), kind=kOutput, calls=%fused_computation.125 | convolution fusion | flops 2415919104 | bytes 9437184 | tf_op jit(solution)/shard_map/dot_general | solution.py:906
  179.2 1.5 multiply_convert_fusion
  180.8 7.7 %select_reduce_fusion.2 = (f32[]{:T(128)}, f32[]{:T(128)}, f32[512]{0:T(512)S(1)}, f32[512]{0:T(512)S(1)}, f32[768]{0:T(1024)S(1)}, /*index=5*/f32[768]{0:T(1024)S(1)}, f32[]{:T(128)}, bf16[512,768]{1,0:T(8,128)(2,1)}) fusion(pred[512]{0:T(512)(128)(4,1)S(1)} %lt.32, f32[512,768]{1,0:T(8,128)S(1)} %get-tuple-element.88, f32[768]{0:T(1024)S(1)} %add.212, ...), kind=kOutput, calls=%fused_computation.37 | convolution fusion | flops 2424567296 | bytes 13390348 | tf_op jit(solution)/shard_map/dot_general | solution.py:906
  188.6 1.8 convert_reduce_fusion.2
  190.4 1.8 convolution_convert_fusion.3
  192.2 0.7 copy-done.19
  193.0 5.0 %convolution_convert_fusion.1 = bf16[768,3072]{1,0:T(8,128)(2,1)} fusion(bf16[512,3072]{1,0:T(8,128)(2,1)S(1)} %copy-done.19, f32[512,768]{1,0:T(8,128)S(1)} %get-tuple-element.88, f32[768]{0:T(1024)S(1)} %add.206, f32[768]{0:T(1024)S(1)} %mul.216, f32[512]{0:T(512)S(1)} %add_rsqrt_fusion.1, f32[512]{0:T(512)S(1)} %broadcast_multiply_fusion.5), kind=kOutput, calls=%fused_computation.20 | convolution fusion | flops 2420244480 | bytes 9447424 | tf_op jit(solution)/shard_map/dot_general | solution.py:906
  198.0 4.4 convolution_convert_fusion
  202.8 2.0 select_maximum_fusion.3
  204.9 0.7 pad.55.clone
  205.6 78.9 %shard_map.280 = (f32[24,768]{1,0:T(8,128)}, f32[24,3072]{1,0:T(8,128)}, f32[96,768]{1,0:T(8,128)}, f32[8,128]{1,0:T(8,128)}, bf16[8,64,768]{2,1,0:T(8,128)(2,1)}) custom-call(bf16[4,4,2,24,768]{4,3,2,1,0:T(8,128)(2,1)} %bitcast.128, bf16[4,4,2,24,3072]{4,3,2,1,0:T(8,128)(2,1)} %bitcast.117, bf16[4,4,2,96,768]{4,3,2,1,0:T(8,128)(2,1)} %bitcast.118, ...), custom_call_target="tpu_custom_call" | custom-call | tf_op jit(solution)/shard_map/pallas_call | solution.py:716
  284.5 0.8 fusion.13
  285.3 1.3 copy.48
  286.6 17.3 %shard_map.281 = bf16[2,2,4,2,64,192]{5,4,3,2,1,0:T(8,128)(2,1)} custom-call(bf16[4,2,4,64,192]{4,3,2,1,0:T(8,128)(2,1)} %bitcast.120), custom_call_target="tpu_custom_call" | custom-call | tf_op jit(solution)/shard_map/pallas_call | solution.py:716
  303.9 46.1 %shard_map.282 = bf16[2048,576]{1,0:T(8,128)(2,1)} custom-call(bf16[3,2048,128]{2,1,0:T(8,128)(2,1)} %get-tuple-element.47.query, bf16[3,2048,128]{2,1,0:T(8,128)(2,1)} %get-tuple-element.48.key, bf16[3,2048,128]{2,1,0:T(8,128)(2,1)} %get-tuple-element.49.value, bf16[2048,192]{1,0:T(8,128)(2,1)} %bitcast.119, f32[2048,192]{1,0:T(8,128)} %get-tuple-element.50.context), custom_call_target="tpu_custom_call" | custom-call | tf_op jit(solution)/shard_map/pallas_call | solution.py:945
  350.1 4.9 %convolution_convert_fusion.4 = bf16[768,576]{0,1:T(8,128)(2,1)} fusion(bf16[2048,768]{1,0:T(8,128)(2,1)S(1)} %copy-done.16, bf16[2048,576]{1,0:T(8,128)(2,1)} %shard_map.282), kind=kOutput, calls=%fused_computation.55 | convolution fusion | flops 1812381696 | bytes 6389760 | tf_op jit(solution)/shard_map/dot_general | solution.py:906
  354.9 2.2 copy.49
  357.1 5.2 %convolution_convert_fusion.2 = bf16[2048,768]{1,0:T(8,128)(2,1)} fusion(bf16[2048,576]{1,0:T(8,128)(2,1)S(1)} %copy-done.1, bf16[768,576]{1,0:T(8,128)(2,1)} %get-tuple-element.51), kind=kOutput, calls=%fused_computation.21 | convolution fusion | flops 1813512192 | bytes 6389760 | tf_op jit(solution)/shard_map/dot_general | solution.py:906
  362.4 32.4 %shard_map.283 = (f32[4,24,576]{2,1,0:T(8,128)}, f32[2,4,64,768]{3,2,1,0:T(8,128)}) custom-call(bf16[2,2,4,2,24,576]{5,4,3,2,1,0:T(8,128)(2,1)} %bitcast.121, bf16[2,2,4,2,64,768]{5,4,3,2,1,0:T(8,128)(2,1)} %bitcast.124), custom_call_target="tpu_custom_call" | custom-call | tf_op jit(solution)/shard_map/pallas_call | solution.py:716
  394.8 0.1 slice.71
  394.9 2.4 multiply_reduce_fusion
  397.3 2.8 fusion.10.grads
  400.1 0.5 convert_reduce_fusion.1
  400.6 0.1 slice_dynamic-update-slice_fusion
  400.8 0.1 reshape.495
  400.9 0.1 slice_dynamic-update-slice_fusion.1
  401.0 0.1 reshape.494
  401.2 0.1 select_maximum_fusion
  401.3 0.7 pad.60.small
  402.0 26.8 %shard_map.284 = (bf16[8,64,768]{2,1,0:T(8,128)(2,1)}, f32[32,8,128]{2,1,0:T(8,128)}) custom-call(bf16[8,64,768]{2,1,0:T(8,128)(2,1)} %fusion.10.grads, f32[32,8,128]{2,1,0:T(8,128)} %pad.60.small), custom_call_target="tpu_custom_call" | custom-call | tf_op jit(solution)/shard_map/pallas_call | solution.py:716
  428.9 1.0 reduce_sum.208
  429.9 0.5 slice_bitcast_fusion.5
  430.4 0.2 reshape.496
  430.6 0.2 copy.54
  430.8 0.9 reshape.497
  431.7 0.5 slice_bitcast_fusion
  432.2 0.5 slice_bitcast_fusion.1
  432.7 0.6 reduce_sum.209
  434.0 0.5 sqrt_bitcast_fusion
  434.5 2.1 copy.73
  436.6 0.9 copy.74
  437.5 0.6 copy.75
  438.1 0.7 copy.76
  438.8 0.7 copy.77
  (74 shorter events, 1.2 us)
Async XLA Ops:
  138.0 5.6 %copy-start.4 = (bf16[4,512,192]{1,2,0:T(8,128)(2,1)}, bf16[4,512,192]{1,2,0:T(8,128)(2,1)S(1)}, u32[]{:S(2)}) copy-start(bf16[4,512,192]{1,2,0:T(8,128)(2,1)S(1)} %copy.46) | copy-start | bytes 2359300
  144.2 8.2 %copy-start = (bf16[8,64,768]{2,1,0:T(8,128)(2,1)S(1)}, bf16[8,64,768]{2,1,0:T(8,128)(2,1)}, u32[]{:S(2)}) copy-start(bf16[8,64,768]{2,1,0:T(8,128)(2,1)} %get-tuple-element.40) | copy-start | bytes 2359300
  144.2 8.4 %copy-start.2 = (bf16[8,64,768]{2,1,0:T(8,128)(2,1)S(1)}, bf16[8,64,768]{2,1,0:T(8,128)(2,1)}, u32[]{:S(2)}) copy-start(bf16[8,64,768]{2,1,0:T(8,128)(2,1)} %get-tuple-element.39) | copy-start | bytes 2359300
  171.9 7.3 %copy-start.18 = (bf16[512,3072]{1,0:T(8,128)(2,1)}, bf16[512,3072]{1,0:T(8,128)(2,1)S(1)}, u32[]{:S(2)}) copy-start(bf16[512,3072]{1,0:T(8,128)(2,1)S(1)} %get-tuple-element.80) | copy-start | bytes 9437188
  171.9 7.3 %slice-start = ((s8[6291456]{0:T(1024)(128)(4,1)}), s8[4194304]{0:T(1024)(128)(4,1)S(1)}, s32[]{:S(2)}) async-start(s8[6291456]{0:T(1024)(128)(4,1)} %bitcast.114), calls=%async_computation | async-start | bytes 8388608
  171.9 7.3 %slice-start.1 = ((s8[6291456]{0:T(1024)(128)(4,1)}), s8[2097152]{0:T(1024)(128)(4,1)S(1)}, s32[]{:S(2)}) async-start(s8[6291456]{0:T(1024)(128)(4,1)} %bitcast.114), calls=%async_computation.1 | async-start | bytes 4194304
  180.8 7.8 %copy-start.6 = (f32[512,768]{1,0:T(8,128)S(1)}, f32[512,768]{1,0:T(8,128)}, u32[]{:S(2)}) copy-start(f32[512,768]{1,0:T(8,128)} %fusion.29) | copy-start | bytes 4718596
  188.6 1.8 copy-start.5
  190.4 1.9 copy-start.8
  190.4 2.6 copy-start.19
  205.6 78.9 %copy-start.7 = (bf16[32,24,768]{2,1,0:T(8,128)(2,1)S(1)}, bf16[32,24,768]{2,1,0:T(8,128)(2,1)}, u32[]{:S(2)}) copy-start(bf16[32,24,768]{2,1,0:T(8,128)(2,1)} %get-tuple-element.41) | copy-start | bytes 3538948
  205.6 78.9 %copy-start.9 = (bf16[512,768]{1,0:T(8,128)(2,1)S(1)}, bf16[512,768]{1,0:T(8,128)(2,1)}, u32[]{:S(2)}) copy-start(bf16[512,768]{1,0:T(8,128)(2,1)} %copy-done.8) | copy-start | bytes 2359300
  303.9 46.2 %copy-start.16 = (bf16[2048,768]{1,0:T(8,128)(2,1)S(1)}, bf16[2048,768]{1,0:T(8,128)(2,1)}, u32[]{:S(2)}) copy-start(bf16[2048,768]{1,0:T(8,128)(2,1)} %get-tuple-element.46) | copy-start | bytes 9437188
  350.0 7.1 %copy-start.1 = (bf16[2048,576]{1,0:T(8,128)(2,1)S(1)}, bf16[2048,576]{1,0:T(8,128)(2,1)}, u32[]{:S(2)}) copy-start(bf16[2048,576]{1,0:T(8,128)(2,1)} %shard_map.282) | copy-start | bytes 7077892
  394.9 2.4 copy-start.3
  400.1 30.3 %copy-start.13 = (f32[4,24,576]{2,1,0:T(8,128)S(1)}, f32[4,24,576]{2,1,0:T(8,128)}, u32[]{:S(2)}) copy-start(f32[4,24,576]{2,1,0:T(8,128)} %get-tuple-element.55) | copy-start | bytes 663556
  400.1 31.6 %copy-start.15 = (f32[8,128]{1,0:T(8,128)S(1)}, f32[8,128]{1,0:T(8,128)}, u32[]{:S(2)}) copy-start(f32[8,128]{1,0:T(8,128)} %get-tuple-element.57) | copy-start | bytes 12292
  400.1 32.6 %copy-start.17 = (s32[8]{0:T(128)S(1)}, s32[8]{0:T(128)}, u32[]{:S(2)}) copy-start(s32[8]{0:T(128)} %param.17) | copy-start | bytes 100
  401.3 36.1 %copy-start.14 = (f32[24,768]{1,0:T(8,128)S(1)}, f32[24,768]{1,0:T(8,128)}, u32[]{:S(2)}) copy-start(f32[24,768]{1,0:T(8,128)} %get-tuple-element.124) | copy-start | bytes 221188
  402.0 36.1 %copy-start.12 = (f32[24,3072]{1,0:T(8,128)S(1)}, f32[24,3072]{1,0:T(8,128)}, u32[]{:S(2)}) copy-start(f32[24,3072]{1,0:T(8,128)} %get-tuple-element.128) | copy-start | bytes 884740
  428.8 7.8 %copy-start.10 = (bf16[8,64,768]{2,1,0:T(8,128)(2,1)S(1)}, bf16[8,64,768]{2,1,0:T(8,128)(2,1)}, u32[]{:S(2)}) copy-start(bf16[8,64,768]{2,1,0:T(8,128)(2,1)} %get-tuple-element.118) | copy-start | bytes 2359300
  428.9 10.0 %copy-start.11 = (f32[96,768]{1,0:T(8,128)S(1)}, f32[96,768]{1,0:T(8,128)}, u32[]{:S(2)}) copy-start(f32[96,768]{1,0:T(8,128)} %get-tuple-element.130) | copy-start | bytes 884740
